TPU v7x, 512 devices: a whole 4x4x16 slice. The times are simulated.
512 devices in a mesh: gx: 16 (over y, x), gy: 32 (over z, core).
Axes of the slice: x: 4, y: 4, z: 16, core: 2. Of those that a mesh axis runs over, the one named last changes fastest.
Arguments:
- tiles: bfloat16 [256, 96, 128, 128], P('gx', 'gy'), may hold values from 0.0099487305 to 1
- tile_cols: int32 [256, 96], P('gx', 'gy'), may hold values from 0 to 7
- row_counts: int32 [256, 32], P('gx', 'gy'), may hold values from 0 to 3
- start_block: bfloat16 [32768, 128], P('gx'), may hold values from -6 to 6
Outputs:
- vectors: bfloat16 [32768, 128], P(('gx', 'gy'))
- col_scales: float32 [2, 128], replicated
Inputs may be any that keep to these rules, and one draw needn't show every extreme that they name: `tile_cols`: a column tile inside the slot's block of columns. `row_counts`: slots at or past the count are ignored.
All inputs are finite; a program needn't handle non-finite values.
Results may differ from a plain program's by a relative error of at most 0.0065.
Values may be sent and summed in bfloat16 or wider, within the bound.
No kernel may reach another device: no remote copies, remote signals or barrier semaphores. Data moves between devices by JAX's collectives and lax.ppermute only.
A program may use at most 64 MiB of HBM per device.

v0:
```python
import functools

import jax
import jax.numpy as jnp
from jax import lax
from jax.sharding import Mesh
from jax.sharding import PartitionSpec as P

GX = ("gx_0", "gx_1")
GY = ("gy_0", "gy_1")
GX_GY = ("gx_0", "gx_1", "gy_0", "gy_1")


def from_everyone(array, axis):
    peers = lax.axis_size(axis)
    return lax.all_to_all(
        jnp.broadcast_to(array[None], (peers, *array.shape)), axis, 0, 0, tiled=True
    )


def over_copies(array, axis):
    return from_everyone(array, axis).sum(axis=0)


def broadcast(array, axis, root):
    return lax.dynamic_index_in_dim(lax.all_gather(array, axis), root, 0, keepdims=False)


def in_blocks(array, dim, peers):
    before, after = (array.shape[:dim], array.shape[dim + 1 :])
    return jnp.moveaxis(array.reshape(*before, peers, -1, *after), dim, 0)


def sum_at_owner(array, axis, dim):
    peers = lax.axis_size(axis)
    tiles = lax.all_to_all(in_blocks(array, dim, peers), axis, 0, 0, tiled=True)
    return jnp.sum(tiles, axis=0)


def by_axis(array, axes):
    return functools.reduce(lax.psum, axes, array)


def on_device(tiles, tile_cols, row_counts, start_block):
    row_tiles = tiles.shape[0]
    slot_count = tiles.shape[1]
    side = tiles.shape[2]
    width = start_block.shape[1]
    groups = lax.axis_size(GX)
    blocks = lax.axis_size(GY)
    col_tiles = row_tiles * groups // blocks
    local_rows = row_tiles * side
    nodes = local_rows * groups
    masks = (jnp.arange(slot_count)[None, :] < row_counts).astype(jnp.bfloat16)
    row_sums = jnp.einsum("rsab,rs->ra", tiles, masks, preferred_element_type=jnp.float32).reshape(
        -1
    )
    degree = 1.0 + over_copies(row_sums, GY)
    scale = 1.0 / jnp.sqrt(degree)
    upd = (scale[:, None] * start_block.astype(jnp.float32)).astype(jnp.bfloat16)
    first_tile = lax.axis_index(GY) * col_tiles
    scales = []
    share = local_rows // blocks
    mine = lax.axis_index(GY) * share
    vectors = upd
    scale_share = lax.dynamic_slice_in_dim(scale, mine, share, 0)
    for step in range(2):
        offset = first_tile % row_tiles * side
        piece = lax.dynamic_slice_in_dim(upd, offset, col_tiles * side, 0)
        column = broadcast(piece, GX, first_tile // row_tiles)
        product_column = column.reshape(col_tiles, side, width)
        picked = product_column[tile_cols] * masks[:, :, None, None]
        total = jnp.einsum("rsab,rsbk->rak", tiles, picked, preferred_element_type=jnp.float32)
        partial_value = sum_at_owner(total.reshape(local_rows, width), GY, 0)
        own_rows = lax.dynamic_slice_in_dim(upd, mine, share, 0).astype(jnp.float32)
        mixed = scale_share[:, None] * (partial_value + own_rows)
        squares = by_axis(jnp.sum(mixed * mixed, axis=0), GX_GY)
        spread = jnp.sqrt(squares / nodes + 1e-06)
        scales.append(spread)
        normed = mixed / spread
        if step == 0:
            upd = lax.all_gather(
                (scale_share[:, None] * normed).astype(jnp.bfloat16), GY, axis=0, tiled=True
            )
        else:
            vectors = normed.astype(jnp.bfloat16)
    return (vectors, jnp.stack(scales))


def solution(mesh):
    torus = Mesh(mesh.devices.reshape(4, 4, 16, 2), ("gx_0", "gx_1", "gy_0", "gy_1"))
    placed = (P(GX, GY, None, None), P(GX, GY), P(GX, GY), P(GX, None))
    return jax.shard_map(
        on_device, mesh=torus, in_specs=placed, out_specs=(P(GX_GY, None), P()), check_vma=False
    )
```

profile of v0, /device:TPU:1, one launch (start us, length us, event | category | flops | bytes accessed | tf_op | source)
XLA Modules:
  0.0 450.5 jit_solution(3904337507445448299)
XLA Ops:
  7.2 0.8 fusion.8
  8.0 1.9 convert_reduce_fusion
  10.0 0.8 broadcast_in_dim.11
  10.9 16.7 %all-to-all-start = ((f32[32,1,2048]{2,1,0:T(1,128)}), f32[32,1,2048]{2,1,0:T(1,128)S(1)}, u32[]{:S(2)}, u32[]{:S(2)}) async-start(f32[32,1,2048]{2,1,0:T(1,128)} %broadcast_in_dim.11), calls=%async_computation | async-start | bytes 524288 | tf_op jit(solution)/shard_map/all_to_all | solution.py:16
  27.7 21.9 %all-to-all-done = f32[32,1,2048]{2,1,0:T(1,128)S(1)} async-done(((f32[32,1,2048]{2,1,0:T(1,128)}), f32[32,1,2048]{2,1,0:T(1,128)S(1)}, u32[]{:S(2)}, u32[]{:S(2)}) %all-to-all-start) | async-done | bytes 262176 | tf_op jit(solution)/shard_map/all_to_all | solution.py:16
  50.1 0.8 copy-done.1
  50.9 0.7 constant_dynamic-slice_fusion.3
  51.9 58.4 %all-gather.5.cloned.1.call-done = bf16[16384,128]{1,0:T(8,128)(2,1)} async-done(((bf16[1024,128]{1,0:T(8,128)(2,1)}), bf16[16384,128]{1,0:T(8,128)(2,1)}) %all-gather.5.cloned.1.call-update) | async-done | bytes 4194320 | tf_op jit(solution)/shard_map/all_gather | solution.py:26
  110.3 1.0 constant_dynamic-slice_fusion.2
  111.3 0.8 gather_fusion
  112.7 1.6 fusion.2
  114.3 13.0 %all-to-all-start.1 = ((f32[32,64,128]{2,1,0:T(8,128)}), f32[32,64,128]{2,1,0:T(8,128)S(1)}, u32[]{:S(2)}, u32[]{:S(2)}) async-start(f32[32,64,128]{2,1,0:T(8,128)} %bitcast.36), calls=%async_computation.1 | async-start | bytes 2097152 | tf_op jit(solution)/shard_map/all_to_all | solution.py:36
  127.5 55.6 %all-to-all-done.1 = f32[32,64,128]{2,1,0:T(8,128)S(1)} async-done(((f32[32,64,128]{2,1,0:T(8,128)}), f32[32,64,128]{2,1,0:T(8,128)S(1)}, u32[]{:S(2)}, u32[]{:S(2)}) %all-to-all-start.1) | async-done | bytes 1048608 | tf_op jit(solution)/shard_map/all_to_all | solution.py:36
  183.1 0.8 multiply_reduce_fusion.1
  183.9 8.4 %psum.56 = f32[128]{0:T(128)S(1)} all-reduce(f32[128]{0:T(128)S(1)} %multiply_reduce_fusion.1), channel_id=1, replica_groups=mesh['gx_0'=4,'gx_1'=4,'gy_0'=16,'gy_1'=2] {'gx_0'}, use_global_device_ids=true, to_apply=%region_4.5 | all-reduce | flops 128 | bytes 1024 | tf_op jit(solution)/shard_map/psum | solution.py:41
  192.3 6.6 %psum.57 = f32[128]{0:T(128)S(1)} all-reduce(f32[128]{0:T(128)S(1)} %psum.56), channel_id=1, replica_groups=mesh['gx_0'=4,'gx_1'=4,'gy_0'=16,'gy_1'=2] {'gx_1'}, use_global_device_ids=true, to_apply=%region_5.6 | all-reduce | flops 128 | bytes 1024 | tf_op jit(solution)/shard_map/psum | solution.py:41
  198.9 20.0 %psum.58 = f32[128]{0:T(128)S(1)} all-reduce(f32[128]{0:T(128)S(1)} %psum.57), channel_id=1, replica_groups=mesh['gx_0'=4,'gx_1'=4,'gy_0'=16,'gy_1'=2] {'gy_0'}, use_global_device_ids=true, to_apply=%region_6.7 | all-reduce | flops 128 | bytes 1024 | tf_op jit(solution)/shard_map/psum | solution.py:41
  218.9 13.6 %psum.59 = f32[128]{0:T(128)S(1)} all-reduce(f32[128]{0:T(128)S(1)} %psum.58), channel_id=1, replica_groups=mesh['gx_0'=4,'gx_1'=4,'gy_0'=16,'gy_1'=2] {'gy_1'}, use_global_device_ids=true, to_apply=%region_7.8 | all-reduce | flops 128 | bytes 1024 | tf_op jit(solution)/shard_map/psum | solution.py:41
  232.6 0.8 multiply_convert_fusion.1
  233.4 30.4 %all_gather.17 = bf16[2048,128]{1,0:T(8,128)(2,1)S(1)} all-gather(bf16[64,128]{1,0:T(8,128)(2,1)S(1)} %multiply_convert_fusion.1), channel_id=1, replica_groups=mesh['gx_0'=4,'gx_1'=4,'gy_0'=16,'gy_1'=2] {'gy_0','gy_1'}, dimensions={0}, use_global_device_ids=true | all-gather | bytes 540672 | tf_op jit(solution)/shard_map/all_gather | solution.py:82
  263.7 0.8 copy-done.2
  264.5 0.7 constant_dynamic-slice_fusion.1
  265.3 55.9 %all-gather.7.cloned.1.call-done = bf16[16384,128]{1,0:T(8,128)(2,1)} async-done(((bf16[1024,128]{1,0:T(8,128)(2,1)}), bf16[16384,128]{1,0:T(8,128)(2,1)}) %all-gather.7.cloned.1.call-update) | async-done | bytes 4194320 | tf_op jit(solution)/shard_map/all_gather | solution.py:26
  321.2 1.0 constant_dynamic-slice_fusion
  322.2 0.8 gather_fusion.1
  323.7 68.5 %all_to_all.16 = f32[32,64,128]{2,1,0:T(8,128)S(1)} all-to-all(f32[32,64,128]{2,1,0:T(8,128)S(1)} %bitcast.37), channel_id=1, replica_groups=mesh['gx_0'=4,'gx_1'=4,'gy_0'=16,'gy_1'=2] {'gy_0','gy_1'}, dimensions={0} | all-to-all | bytes 2097152 | tf_op jit(solution)/shard_map/all_to_all | solution.py:36
  392.3 0.8 multiply_reduce_fusion
  393.1 8.4 %psum.60 = f32[128]{0:T(128)S(1)} all-reduce(f32[128]{0:T(128)S(1)} %multiply_reduce_fusion), channel_id=1, replica_groups=mesh['gx_0'=4,'gx_1'=4,'gy_0'=16,'gy_1'=2] {'gx_0'}, use_global_device_ids=true, to_apply=%region_10.11 | all-reduce | flops 128 | bytes 1024 | tf_op jit(solution)/shard_map/psum | solution.py:41
  401.5 6.6 %psum.61 = f32[128]{0:T(128)S(1)} all-reduce(f32[128]{0:T(128)S(1)} %psum.60), channel_id=1, replica_groups=mesh['gx_0'=4,'gx_1'=4,'gy_0'=16,'gy_1'=2] {'gx_1'}, use_global_device_ids=true, to_apply=%region_11.12 | all-reduce | flops 128 | bytes 1024 | tf_op jit(solution)/shard_map/psum | solution.py:41
  408.0 20.0 %psum.62 = f32[128]{0:T(128)S(1)} all-reduce(f32[128]{0:T(128)S(1)} %psum.61), channel_id=1, replica_groups=mesh['gx_0'=4,'gx_1'=4,'gy_0'=16,'gy_1'=2] {'gy_0'}, use_global_device_ids=true, to_apply=%region_12.13 | all-reduce | flops 128 | bytes 1024 | tf_op jit(solution)/shard_map/psum | solution.py:41
  428.1 13.6 %psum.63 = f32[128]{0:T(128)S(1)} all-reduce(f32[128]{0:T(128)S(1)} %psum.62), channel_id=1, replica_groups=mesh['gx_0'=4,'gx_1'=4,'gy_0'=16,'gy_1'=2] {'gy_1'}, use_global_device_ids=true, to_apply=%region_13.14 | all-reduce | flops 128 | bytes 1024 | tf_op jit(solution)/shard_map/psum | solution.py:41
  441.7 1.4 divide_convert_fusion
  (27 shorter events, 3.0 us)
Async XLA Ops:
  7.2 42.6 %copy-start.3 = (bf16[2048,128]{1,0:T(8,128)(2,1)S(1)}, bf16[2048,128]{1,0:T(8,128)(2,1)}, u32[]{:S(2)}) copy-start(bf16[2048,128]{1,0:T(8,128)(2,1)} %param.7) | copy-start | bytes 1572868
  9.9 41.8 %copy-start.4 = (s32[16,3]{0,1:T(4,128)S(1)}, s32[16,3]{0,1:T(4,128)}, u32[]{:S(2)}) copy-start(s32[16,3]{0,1:T(4,128)} %param.5) | copy-start | bytes 580
  10.9 38.7 %all-to-all-start = ((f32[32,1,2048]{2,1,0:T(1,128)}), f32[32,1,2048]{2,1,0:T(1,128)S(1)}, u32[]{:S(2)}, u32[]{:S(2)}) async-start(f32[32,1,2048]{2,1,0:T(1,128)} %broadcast_in_dim.11), calls=%async_computation | async-start | bytes 524288 | tf_op jit(solution)/shard_map/all_to_all | solution.py:16
  27.6 82.7 %all-gather.5.cloned.1.call-start = ((), (), s32[]{:S(2)}) async-start(), calls=%async_computation.3 | async-start | bytes 4456448 | tf_op jit(solution)/shard_map/all_gather | solution.py:26
  50.1 0.8 copy-start.1
  111.3 1.4 copy-start
  114.3 68.7 %all-to-all-start.1 = ((f32[32,64,128]{2,1,0:T(8,128)}), f32[32,64,128]{2,1,0:T(8,128)S(1)}, u32[]{:S(2)}, u32[]{:S(2)}) async-start(f32[32,64,128]{2,1,0:T(8,128)} %bitcast.36), calls=%async_computation.1 | async-start | bytes 2097152 | tf_op jit(solution)/shard_map/all_to_all | solution.py:36
  127.3 193.9 %all-gather.7.cloned.1.call-start = ((), (), s32[]{:S(2)}) async-start(), calls=%async_computation.4 | async-start | bytes 4456448 | tf_op jit(solution)/shard_map/all_gather | solution.py:26
  263.7 0.8 copy-start.2
Sparse Core Ops, SparseCore 0:
  51.8 58.4 all-gather.4
  265.4 55.7 all-gather.6
where the time goes:
time: 451 us
  blocking collectives  196 us (43%)
  waiting for transfers between devices  192 us (43%)
  starting transfers between devices  29.8 us (7%)
  between operations  14.2 us (3%)
  local copies, waits for them, and re-layouts  8.3 us (2%)
  other arithmetic  7.77 us (2%)
    all_gather x2, waiting for transfers between devices, broadcast(): lax.all_gather(array, axis)  114 us
    psum x8, blocking collectives, by_axis(): return functools.reduce(lax.psum, axes, array)  97.2 us
    all_to_all x1, blocking collectives, sum_at_owner(): tiles = lax.all_to_all(in_blocks(array, dim, peers), axis, 0, 0, tiled=True)  68.5 us
    all_to_all x1, waiting for transfers between devices, sum_at_owner(): tiles = lax.all_to_all(in_blocks(array, dim, peers), axis, 0, 0, tiled=True)  55.6 us
    all_gather x1, blocking collectives, on_device(): lax.all_gather((scale_share[:, None] * normed).astype(jnp.bfloat16), GY,...  30.4 us
    all_to_all x1, waiting for transfers between devices, from_everyone(): lax.all_to_all(jnp.broadcast_to(array[None], (peers, *array.shape)), axis...  21.9 us
    all_to_all x1, starting transfers between devices, from_everyone(): lax.all_to_all(jnp.broadcast_to(array[None], (peers, *array.shape)), axis...  16.7 us
    all_to_all x1, starting transfers between devices, sum_at_owner(): tiles = lax.all_to_all(in_blocks(array, dim, peers), axis, 0, 0, tiled=True)  13 us
  transfers between devices with their start and end apart: 4, of which 4 were waited for; matrix products, arithmetic and copies ran while one was open for 0% of the time, Pallas kernels for 0%

commit v1 on v0

v1 whole, which is shorter than its diff:
```python
import jax
import jax.numpy as jnp
from jax import lax
from jax.experimental import pallas as pl
from jax.experimental.pallas import tpu as pltpu
from jax.sharding import Mesh
from jax.sharding import PartitionSpec as P

GX = ("gx_0", "gx_1")
GY = ("gy_0", "gy_1")
EVERY = ("gx_0", "gx_1", "gy_0", "gy_1")
Z = "gy_0"
CORE = "gy_1"
PLANE = ("gx_0", "gx_1", "gy_1")


def exchange(array, axis):
    return lax.all_to_all(array, axis, 0, 0, tiled=True)


def from_everyone(array, axis):
    peers = lax.axis_size(axis)
    return exchange(jnp.broadcast_to(array[None], (peers, *array.shape)), axis)


def transpose_planes(array):
    n = lax.axis_size(GX)
    perm = [
        ((i * n + z) * 2 + c, (z * n + i) * 2 + c)
        for i in range(n)
        for z in range(n)
        for c in range(2)
    ]
    return lax.ppermute(array, EVERY, perm)


def row_sum_kernel(counts, tiles, out):
    row_tiles, slots, side, _ = tiles.shape
    for r in range(row_tiles):
        wide = jnp.concatenate([tiles[r, s] for s in range(slots)], axis=1)
        slot = lax.broadcasted_iota(jnp.int32, (8, slots * side), 1) // side
        live = jnp.where(slot < counts[r, 0], 1.0, 0.0).astype(tiles.dtype)
        sums = lax.dot_general(
            live, wide, (((1,), (1,)), ((), ())), preferred_element_type=jnp.float32
        )
        out[r : r + 1] = sums[0:1]


def pick(cols, counts, column, r, slots, side):
    parts = []
    for s in range(slots):
        start = pl.multiple_of(cols[r, s] * side, side)
        part = column[pl.ds(start, side), :]
        parts.append(jnp.where(s < counts[r, 0], part, jnp.zeros_like(part)))
    return jnp.concatenate(parts, axis=0)


def first_kernel(place, cols, counts, tiles, start, scale, mine, other, column):
    row_tiles, slots, side, _ = tiles.shape
    half = row_tiles // 2
    spread = jnp.transpose(scale[...])
    for t in range(half):
        rows = slice(t * side, (t + 1) * side)
        value = start[rows, :].astype(jnp.float32) * spread[:, t : t + 1]
        column[rows, :] = value.astype(column.dtype)
    for out, core in ((other, 1 - place[0]), (mine, place[0])):
        for t in range(half):
            r = core * half + t
            wide = jnp.concatenate([tiles[r, s] for s in range(slots)], axis=1)
            out[t * side : (t + 1) * side, :] = jnp.dot(
                wide,
                pick(cols, counts, column, r, slots, side),
                preferred_element_type=jnp.float32,
            )


def second_kernel(place, cols, counts, tiles, column, mine, other):
    row_tiles, slots, side, _ = tiles.shape
    half = row_tiles // 2
    share = side // 2
    core = place[0]
    for r in range(row_tiles):
        picked = pick(cols, counts, column, r, slots, side)
        diagonal = (place[1] == place[2]) & (core == r // half)
        for out, part in ((other, 1 - core), (mine, core)):
            rows = pl.ds(pl.multiple_of(part * share, share), share)
            wide = jnp.concatenate([tiles[r, s, rows, :] for s in range(slots)], axis=1)
            own = column[pl.ds((r % half) * side + part * share, share), :]
            value = jnp.dot(wide, picked, preferred_element_type=jnp.float32)
            value = value + jnp.where(diagonal, own.astype(jnp.float32), 0.0)
            out[r * share : (r + 1) * share, :] = value


SMEM = pl.BlockSpec(memory_space=pltpu.SMEM)
VMEM = pl.BlockSpec(memory_space=pltpu.VMEM)
PARAMS = pltpu.CompilerParams(vmem_limit_bytes=24 << 20)


def on_device(tiles, tile_cols, row_counts, start_block):
    row_tiles, slot_count, side, _ = tiles.shape
    width = start_block.shape[1]
    groups = lax.axis_size(GX)
    half_tiles = row_tiles // 2
    local_rows = row_tiles * side
    half_rows = local_rows // 2
    share = half_rows // groups
    nodes = local_rows * groups
    core = lax.axis_index(CORE)
    line = lax.axis_index(GX)
    plane = lax.axis_index(Z)
    f32, bf16 = jnp.float32, jnp.bfloat16

    start_col = transpose_planes(
        lax.dynamic_slice_in_dim(start_block, core * half_rows, half_rows, 0)
    )

    place = jnp.stack([core, line, plane]).astype(jnp.int32)
    row_sums = pl.pallas_call(
        row_sum_kernel,
        out_shape=jax.ShapeDtypeStruct((row_tiles, side), f32),
        in_specs=[SMEM, VMEM],
        out_specs=VMEM,
        compiler_params=PARAMS,
    )(row_counts, tiles)

    sent = jnp.broadcast_to(row_sums[None], (2 * groups, row_tiles, side))
    got = exchange(sent, PLANE).reshape(groups, 2, row_tiles, side).sum(axis=1)
    of_half = lax.dynamic_slice_in_dim(got, core * half_tiles, half_tiles, 1)
    of_line = lax.dynamic_index_in_dim(got, line, 0, keepdims=False)[:, None, :]
    both = exchange(jnp.concatenate([of_half, of_line], axis=1), Z).sum(axis=0)
    scale_all = 1.0 / jnp.sqrt(1.0 + both)
    scale_col = scale_all[:half_tiles]
    scale_own = lax.dynamic_slice_in_dim(scale_all[half_tiles], core * share, share, 0)
    scale_seg = lax.dynamic_slice_in_dim(
        scale_col.reshape(half_rows), line * share, share, 0
    )

    halves = [jax.ShapeDtypeStruct((half_rows, width), f32)] * 2

    def pair_sum(mine, other):
        return mine + lax.ppermute(other, CORE, [(0, 1), (1, 0)])

    pair = pair_sum(
        *pl.pallas_call(
            first_kernel,
            out_shape=halves,
            in_specs=[SMEM] * 3 + [VMEM] * 3,
            out_specs=[VMEM] * 2,
            scratch_shapes=[pltpu.VMEM((half_rows, width), bf16)],
            compiler_params=PARAMS,
        )(place, tile_cols, row_counts, tiles, start_col, scale_col)
    )
    chunks = pair.astype(bf16).reshape(groups, share, width)
    product = exchange(exchange(chunks, GX), Z).astype(f32).sum(axis=0)
    u_seg = lax.dynamic_slice_in_dim(start_col, line * share, share, 0).astype(f32)
    u_seg = (scale_seg[:, None] * u_seg).astype(bf16).astype(f32)
    w1 = scale_seg[:, None] * (product + u_seg)
    squares1 = jnp.sum(w1 * w1, axis=0)

    v_seg = (scale_seg[:, None] * w1).astype(bf16)
    v = from_everyone(v_seg, GX).reshape(half_rows, width)
    pair = pair_sum(
        *pl.pallas_call(
            second_kernel,
            out_shape=halves,
            in_specs=[SMEM] * 3 + [VMEM] * 2,
            out_specs=[VMEM] * 2,
            compiler_params=PARAMS,
        )(place, tile_cols, row_counts, tiles, v)
    ).reshape(row_tiles, share, width)
    product = exchange(pair.astype(bf16), Z).astype(f32).sum(axis=0)
    w2 = scale_own[:, None] * product
    squares2 = jnp.sum(w2 * w2, axis=0)

    squares = jnp.stack([squares1, squares2])
    squares = from_everyone(squares, PLANE).sum(axis=0)
    squares = from_everyone(squares, Z).sum(axis=0)
    spread1 = jnp.sqrt(squares[0] / nodes + 1e-06)
    spread2 = jnp.sqrt(squares[1] / (spread1 * spread1) / nodes + 1e-06)
    vectors = (w2 / (spread1 * spread2)).astype(bf16)
    return (vectors, jnp.stack([spread1, spread2]))


def solution(mesh):
    torus = Mesh(mesh.devices.reshape(4, 4, 16, 2), EVERY)
    placed = (P(GX, GY, None, None), P(GX, GY), P(GX, GY), P(GX, None))
    return jax.shard_map(
        on_device,
        mesh=torus,
        in_specs=placed,
        out_specs=(P(EVERY, None), P()),
        check_vma=False,
    )
```

time: 451 us -> 220 us (0.49)
  waiting for transfers between devices: 192 us -> 49.9 us
  blocking collectives: 196 us -> 103 us
  starting transfers between devices: 29.8 us -> 53.4 us
  between operations: 14.2 us -> 0.82 us
  local copies, waits for them, and re-layouts: 8.3 us -> 3.3 us
  Pallas kernels: 0 us -> 4.56 us
  other arithmetic: 7.77 us -> 3.24 us
    all_gather x2 -> x0, waiting for transfers between devices: 114 us -> none  [broadcast(): lax.all_gather(array, axis)]
    psum x8 -> x0, blocking collectives: 97.2 us -> none  [by_axis(): return functools.reduce(lax.psum, axes, array)]
    all_to_all x1 -> x4, blocking collectives: 68.5 us -> 103 us  [exchange(): return lax.all_to_all(array, axis, 0, 0, tiled=True)]
    all_to_all x2 -> x4, waiting for transfers between devices: 77.5 us -> 46.9 us  [exchange(): return lax.all_to_all(array, axis, 0, 0, tiled=True)]
    all_gather x1 -> x0, blocking collectives: 30.4 us -> none  [on_device(): lax.all_gather((scale_share[:, None] * normed).astype(jnp.bfloat16), GY,...]
    ppermute x0 -> x3, starting transfers between devices: none -> 16.2 us  [the longest x2 15.5 us: pair_sum(): return mine + lax.ppermute(other, CORE, [(0, 1), (1, 0)])]
    all_to_all x2 -> x4, starting transfers between devices: 29.8 us -> 37.2 us  [exchange(): return lax.all_to_all(array, axis, 0, 0, tiled=True)]
    pallas_call x0 -> x3, Pallas kernels: none -> 4.56 us  [the longest x1 1.7 us: on_device(): pl.pallas_call(first_kernel, out_shape=halves, in_specs=[SMEM] * 3 + [VME...]
  transfers between devices with their start and end apart: 4 -> 7, of which waited for: 4 -> 6; matrix products, arithmetic and copies ran while one was open for 0% -> 0% of each run, Pallas kernels for 0% -> 0%
where the time goes in v1:
time: 220 us; the launch traced here: 219 us
  blocking collectives  103 us (47%)
  starting transfers between devices  53.4 us (24%)
  waiting for transfers between devices  49.9 us (23%)
  Pallas kernels  4.56 us (2%)
  local copies, waits for them, and re-layouts  3.3 us (2%)
  other arithmetic  3.24 us (1%)
    all_to_all x4, blocking collectives, exchange(): return lax.all_to_all(array, axis, 0, 0, tiled=True)  103 us
    all_to_all x4, waiting for transfers between devices, exchange(): return lax.all_to_all(array, axis, 0, 0, tiled=True)  46.9 us
    all_to_all x4, starting transfers between devices, exchange(): return lax.all_to_all(array, axis, 0, 0, tiled=True)  37.2 us
    ppermute x2, starting transfers between devices, pair_sum(): return mine + lax.ppermute(other, CORE, [(0, 1), (1, 0)])  15.5 us
  transfers between devices with their start and end apart: 7, of which 6 were waited for; matrix products, arithmetic and copies ran while one was open for 0% of the time, Pallas kernels for 0%

profile of v1, /device:TPU:1, one launch (start us, length us, event | category | flops | bytes accessed | tf_op | source)
XLA Modules:
  0.0 218.8 jit_solution(1534999061007505891)
XLA Ops:
  0.6 0.8 copy.17.counts
  1.4 1.4 copy-done.1
  2.8 1.3 shard_map.59
  4.2 0.7 broadcast_in_dim.10
  4.9 10.4 %all-to-all-start = ((f32[32,16,128]{2,1,0:T(8,128)}), f32[32,16,128]{2,1,0:T(8,128)S(1)}, u32[]{:S(2)}, u32[]{:S(2)}) async-start(f32[32,16,128]{2,1,0:T(8,128)} %broadcast_in_dim.10), calls=%async_computation | async-start | bytes 524288 | tf_op jit(solution)/shard_map/all_to_all | solution.py:18
  15.3 9.0 %all-to-all-done = f32[32,16,128]{2,1,0:T(8,128)S(1)} async-done(((f32[32,16,128]{2,1,0:T(8,128)}), f32[32,16,128]{2,1,0:T(8,128)S(1)}, u32[]{:S(2)}, u32[]{:S(2)}) %all-to-all-start) | async-done | bytes 262176 | tf_op jit(solution)/shard_map/all_to_all | solution.py:18
  24.4 0.6 pad_maximum_fusion
  25.0 13.0 %all-to-all-start.1 = ((f32[16,9,128]{2,1,0:T(8,128)}), f32[16,9,128]{2,1,0:T(8,128)S(1)}, u32[]{:S(2)}, u32[]{:S(2)}) async-start(f32[16,9,128]{2,1,0:T(8,128)} %pad_maximum_fusion), calls=%async_computation.1 | async-start | bytes 262144 | tf_op jit(solution)/shard_map/all_to_all | solution.py:18
  38.1 0.7 collective-permute-start
  38.8 0.1 copy.21.cols
  38.9 11.3 %all-to-all-done.1 = f32[16,9,128]{2,1,0:T(8,128)S(1)} async-done(((f32[16,9,128]{2,1,0:T(8,128)}), f32[16,9,128]{2,1,0:T(8,128)S(1)}, u32[]{:S(2)}, u32[]{:S(2)}) %all-to-all-start.1) | async-done | bytes 73760 | tf_op jit(solution)/shard_map/all_to_all | solution.py:18
  50.3 1.7 shard_map.60
  52.0 5.7 %collective-permute-start.1 = (f32[1024,128]{1,0:T(8,128)S(1)}, f32[1024,128]{1,0:T(8,128)S(1)}, u32[]{:S(2)}, u32[]{:S(2)}) collective-permute-start(f32[1024,128]{1,0:T(8,128)S(1)} %get-tuple-element.7), channel_id=1, source_target_pairs={{0,1},{1,0},{2,3},{3,2},{4,5},{5,4},{6,7},{7,6},{8,9},{9,8},{10,11... | collective-permute-start | bytes 1572872 | tf_op jit(solution)/shard_map/ppermute | solution.py:141
  57.6 1.5 collective-permute-done.1
  59.2 61.1 %all_to_all.40 = bf16[16,64,128]{2,1,0:T(8,128)(2,1)} all-to-all(bf16[16,64,128]{2,1,0:T(8,128)(2,1)S(1)} %bitcast.18), channel_id=1, replica_groups=mesh['gx_0'=4,'gx_1'=4,'gy_0'=16,'gy_1'=2] {'gx_0','gx_1'}, dimensions={0} | all-to-all | bytes 524288 | tf_op jit(solution)/shard_map/all_to_all | solution.py:18
  120.3 8.6 %all-to-all-start.3 = ((bf16[16,64,128]{2,1,0:T(8,128)(2,1)}), bf16[16,64,128]{2,1,0:T(8,128)(2,1)S(1)}, u32[]{:S(2)}, u32[]{:S(2)}) async-start(bf16[16,64,128]{2,1,0:T(8,128)(2,1)} %all_to_all.40), calls=%async_computation.3 | async-start | bytes 524288 | tf_op jit(solution)/shard_map/all_to_all | solution.py:18
  128.9 0.1 dynamic_slice.22
  129.0 12.7 %all-to-all-done.3 = bf16[16,64,128]{2,1,0:T(8,128)(2,1)S(1)} async-done(((bf16[16,64,128]{2,1,0:T(8,128)(2,1)}), bf16[16,64,128]{2,1,0:T(8,128)(2,1)S(1)}, u32[]{:S(2)}, u32[]{:S(2)}) %all-to-all-start.3) | async-done | bytes 262176 | tf_op jit(solution)/shard_map/all_to_all | solution.py:18
  141.7 0.1 multiply_reduce_fusion.1
  141.9 10.1 %all_to_all.41 = bf16[16,64,128]{2,1,0:T(8,128)(2,1)S(1)} all-to-all(bf16[16,64,128]{2,1,0:T(8,128)(2,1)S(1)} %broadcast_in_dim.12), channel_id=1, replica_groups=mesh['gx_0'=4,'gx_1'=4,'gy_0'=16,'gy_1'=2] {'gx_0','gx_1'}, dimensions={0} | all-to-all | bytes 524288 | tf_op jit(solution)/shard_map/all_to_all | solution.py:18
  152.0 1.6 shard_map.61
  153.6 9.9 %collective-permute-start.2 = (f32[1024,128]{1,0:T(8,128)S(1)}, f32[1024,128]{1,0:T(8,128)S(1)}, u32[]{:S(2)}, u32[]{:S(2)}) collective-permute-start(f32[1024,128]{1,0:T(8,128)S(1)} %get-tuple-element.9), channel_id=1, source_target_pairs={{0,1},{1,0},{2,3},{3,2},{4,5},{5,4},{6,7},{7,6},{8,9},{9,8},{10,11... | collective-permute-start | bytes 1572872 | tf_op jit(solution)/shard_map/ppermute | solution.py:141
  163.5 1.5 collective-permute-done.2
  165.0 0.7 add_convert_fusion
  165.7 5.3 %all-to-all-start.5 = ((bf16[16,64,128]{2,1,0:T(8,128)(2,1)}), bf16[16,64,128]{2,1,0:T(8,128)(2,1)S(1)}, u32[]{:S(2)}, u32[]{:S(2)}) async-start(bf16[16,64,128]{2,1,0:T(8,128)(2,1)} %bitcast.9), calls=%async_computation.5 | async-start | bytes 524288 | tf_op jit(solution)/shard_map/all_to_all | solution.py:18
  171.0 0.1 fusion
  171.1 13.9 %all-to-all-done.5 = bf16[16,64,128]{2,1,0:T(8,128)(2,1)S(1)} async-done(((bf16[16,64,128]{2,1,0:T(8,128)(2,1)}), bf16[16,64,128]{2,1,0:T(8,128)(2,1)S(1)}, u32[]{:S(2)}, u32[]{:S(2)}) %all-to-all-start.5) | async-done | bytes 262176 | tf_op jit(solution)/shard_map/all_to_all | solution.py:18
  185.1 0.1 multiply_reduce_fusion
  185.2 15.4 %all_to_all.42 = f32[32,2,128]{2,1,0:T(2,128)S(1)} all-to-all(f32[32,2,128]{2,1,0:T(2,128)S(1)} %broadcast_in_dim.13), channel_id=1, replica_groups=mesh['gx_0'=4,'gx_1'=4,'gy_0'=16,'gy_1'=2] {'gx_0','gx_1','gy_1'}, dimensions={0} | all-to-all | bytes 65536 | tf_op jit(solution)/shard_map/all_to_all | solution.py:18
  200.6 16.8 %all_to_all.43 = f32[16,2,128]{2,1,0:T(2,128)S(1)} all-to-all(f32[16,2,128]{2,1,0:T(2,128)S(1)} %broadcast_in_dim.14), channel_id=1, replica_groups=mesh['gx_0'=4,'gx_1'=4,'gy_0'=16,'gy_1'=2] {'gy_0'}, dimensions={0} | all-to-all | bytes 32768 | tf_op jit(solution)/shard_map/all_to_all | solution.py:18
  217.5 0.7 divide_convert_fusion
  218.2 0.6 pad_maximum_fusion.2
  (27 shorter events, 0.5 us)
Async XLA Ops:
  0.6 37.4 %copy-start = (bf16[2048,128]{1,0:T(8,128)(2,1)S(1)}, bf16[2048,128]{1,0:T(8,128)(2,1)}, u32[]{:S(2)}) copy-start(bf16[2048,128]{1,0:T(8,128)(2,1)} %param.7) | copy-start | bytes 1572868
  1.4 1.4 copy-start.1
  4.1 34.6 %copy-start.3 = (s32[16,3]{0,1:T(4,128)S(1)}, s32[16,3]{0,1:T(4,128)}, u32[]{:S(2)}) copy-start(s32[16,3]{0,1:T(4,128)} %param.5) | copy-start | bytes 580
  4.2 46.1 %copy-start.2 = (bf16[16,3,128,128]{3,2,1,0:T(8,128)(2,1)S(1)}, bf16[16,3,128,128]{3,2,1,0:T(8,128)(2,1)}, u32[]{:S(2)}) copy-start(bf16[16,3,128,128]{3,2,1,0:T(8,128)(2,1)} %tiles.5) | copy-start | bytes 4718596
  4.9 19.4 %all-to-all-start = ((f32[32,16,128]{2,1,0:T(8,128)}), f32[32,16,128]{2,1,0:T(8,128)S(1)}, u32[]{:S(2)}, u32[]{:S(2)}) async-start(f32[32,16,128]{2,1,0:T(8,128)} %broadcast_in_dim.10), calls=%async_computation | async-start | bytes 524288 | tf_op jit(solution)/shard_map/all_to_all | solution.py:18
  25.0 25.2 %all-to-all-start.1 = ((f32[16,9,128]{2,1,0:T(8,128)}), f32[16,9,128]{2,1,0:T(8,128)S(1)}, u32[]{:S(2)}, u32[]{:S(2)}) async-start(f32[16,9,128]{2,1,0:T(8,128)} %pad_maximum_fusion), calls=%async_computation.1 | async-start | bytes 262144 | tf_op jit(solution)/shard_map/all_to_all | solution.py:18
  38.1 12.2 %collective-permute-start = (bf16[1024,128]{1,0:T(8,128)(2,1)S(1)}, bf16[1024,128]{1,0:T(8,128)(2,1)S(1)}, u32[]{:S(2)}, u32[]{:S(2)}) collective-permute-start(bf16[1024,128]{1,0:T(8,128)(2,1)S(1)} %constant_dynamic-slice_fusion), channel_id=1, source_target_pairs={{0,0},{1,1},{2,32},{3,33},{4,64},{5,65},{6,96},{7,97},{8,128},{9,1... | collective-permute-start | bytes 786440 | tf_op jit(solution)/shard_map/ppermute | solution.py:34
  52.0 7.2 %collective-permute-start.1 = (f32[1024,128]{1,0:T(8,128)S(1)}, f32[1024,128]{1,0:T(8,128)S(1)}, u32[]{:S(2)}, u32[]{:S(2)}) collective-permute-start(f32[1024,128]{1,0:T(8,128)S(1)} %get-tuple-element.7), channel_id=1, source_target_pairs={{0,1},{1,0},{2,3},{3,2},{4,5},{5,4},{6,7},{7,6},{8,9},{9,8},{10,11... | collective-permute-start | bytes 1572872 | tf_op jit(solution)/shard_map/ppermute | solution.py:141
  120.3 21.4 %all-to-all-start.3 = ((bf16[16,64,128]{2,1,0:T(8,128)(2,1)}), bf16[16,64,128]{2,1,0:T(8,128)(2,1)S(1)}, u32[]{:S(2)}, u32[]{:S(2)}) async-start(bf16[16,64,128]{2,1,0:T(8,128)(2,1)} %all_to_all.40), calls=%async_computation.3 | async-start | bytes 524288 | tf_op jit(solution)/shard_map/all_to_all | solution.py:18
  153.6 11.4 %collective-permute-start.2 = (f32[1024,128]{1,0:T(8,128)S(1)}, f32[1024,128]{1,0:T(8,128)S(1)}, u32[]{:S(2)}, u32[]{:S(2)}) collective-permute-start(f32[1024,128]{1,0:T(8,128)S(1)} %get-tuple-element.9), channel_id=1, source_target_pairs={{0,1},{1,0},{2,3},{3,2},{4,5},{5,4},{6,7},{7,6},{8,9},{9,8},{10,11... | collective-permute-start | bytes 1572872 | tf_op jit(solution)/shard_map/ppermute | solution.py:141
  165.7 19.3 %all-to-all-start.5 = ((bf16[16,64,128]{2,1,0:T(8,128)(2,1)}), bf16[16,64,128]{2,1,0:T(8,128)(2,1)S(1)}, u32[]{:S(2)}, u32[]{:S(2)}) async-start(bf16[16,64,128]{2,1,0:T(8,128)(2,1)} %bitcast.9), calls=%async_computation.5 | async-start | bytes 524288 | tf_op jit(solution)/shard_map/all_to_all | solution.py:18

commit v2 on v1

--- a/solution.py
+++ b/solution.py
@@ -23,17 +23,6 @@
     return exchange(jnp.broadcast_to(array[None], (peers, *array.shape)), axis)
 
 
-def transpose_planes(array):
-    n = lax.axis_size(GX)
-    perm = [
-        ((i * n + z) * 2 + c, (z * n + i) * 2 + c)
-        for i in range(n)
-        for z in range(n)
-        for c in range(2)
-    ]
-    return lax.ppermute(array, EVERY, perm)
-
-
 def row_sum_kernel(counts, tiles, out):
     row_tiles, slots, side, _ = tiles.shape
     for r in range(row_tiles):
@@ -55,14 +44,9 @@
     return jnp.concatenate(parts, axis=0)
 
 
-def first_kernel(place, cols, counts, tiles, start, scale, mine, other, column):
+def first_kernel(place, cols, counts, tiles, column, mine, other):
     row_tiles, slots, side, _ = tiles.shape
     half = row_tiles // 2
-    spread = jnp.transpose(scale[...])
-    for t in range(half):
-        rows = slice(t * side, (t + 1) * side)
-        value = start[rows, :].astype(jnp.float32) * spread[:, t : t + 1]
-        column[rows, :] = value.astype(column.dtype)
     for out, core in ((other, 1 - place[0]), (mine, place[0])):
         for t in range(half):
             r = core * half + t
@@ -110,10 +94,6 @@
     plane = lax.axis_index(Z)
     f32, bf16 = jnp.float32, jnp.bfloat16
 
-    start_col = transpose_planes(
-        lax.dynamic_slice_in_dim(start_block, core * half_rows, half_rows, 0)
-    )
-
     place = jnp.stack([core, line, plane]).astype(jnp.int32)
     row_sums = pl.pallas_call(
         row_sum_kernel,
@@ -123,38 +103,46 @@
         compiler_params=PARAMS,
     )(row_counts, tiles)
 
-    sent = jnp.broadcast_to(row_sums[None], (2 * groups, row_tiles, side))
-    got = exchange(sent, PLANE).reshape(groups, 2, row_tiles, side).sum(axis=1)
-    of_half = lax.dynamic_slice_in_dim(got, core * half_tiles, half_tiles, 1)
-    of_line = lax.dynamic_index_in_dim(got, line, 0, keepdims=False)[:, None, :]
-    both = exchange(jnp.concatenate([of_half, of_line], axis=1), Z).sum(axis=0)
-    scale_all = 1.0 / jnp.sqrt(1.0 + both)
-    scale_col = scale_all[:half_tiles]
-    scale_own = lax.dynamic_slice_in_dim(scale_all[half_tiles], core * share, share, 0)
-    scale_seg = lax.dynamic_slice_in_dim(
-        scale_col.reshape(half_rows), line * share, share, 0
-    )
+    def swapped(array):
+        return lax.ppermute(array, CORE, [(0, 1), (1, 0)])
+
+    row_sums = row_sums + swapped(row_sums)
+    start_half = lax.dynamic_slice_in_dim(start_block, core * half_rows, half_rows, 0)
+    part = lax.dynamic_slice_in_dim(row_sums, core * half_tiles, half_tiles, 0)
+    part = jnp.repeat(part, 2, axis=0)
+    high = lax.reduce_precision(part, 8, 7)
+    middle = lax.reduce_precision(part - high, 8, 7)
+    terms = jnp.stack([high, middle, part - high - middle], axis=1).astype(bf16)
+    terms = jnp.pad(terms, ((0, 0), (0, 13), (0, 0)))
+    sent = [start_half.reshape(groups, share, width), terms]
+    got = exchange(jnp.concatenate(sent, axis=1), GX)
+    start_seg = lax.dynamic_index_in_dim(got, plane, 0, keepdims=False)[:share]
+    part = got[:, share : share + 3].astype(f32).sum(axis=1)
+
+    degree = 1.0 + exchange(jnp.stack([part, row_sums], axis=1), Z).sum(axis=0)
+    scale = 1.0 / jnp.sqrt(degree)
+    scale_seg = lax.dynamic_slice_in_dim(scale[0], line % 2 * share, share, 0)
+    scale_own = lax.dynamic_slice_in_dim(scale[1], core * share, share, 0)
 
     halves = [jax.ShapeDtypeStruct((half_rows, width), f32)] * 2
 
     def pair_sum(mine, other):
-        return mine + lax.ppermute(other, CORE, [(0, 1), (1, 0)])
+        return mine + swapped(other)
 
+    u_seg = (scale_seg[:, None] * start_seg.astype(f32)).astype(bf16)
+    u = from_everyone(u_seg, GX).reshape(half_rows, width)
     pair = pair_sum(
         *pl.pallas_call(
             first_kernel,
             out_shape=halves,
-            in_specs=[SMEM] * 3 + [VMEM] * 3,
+            in_specs=[SMEM] * 3 + [VMEM] * 2,
             out_specs=[VMEM] * 2,
-            scratch_shapes=[pltpu.VMEM((half_rows, width), bf16)],
             compiler_params=PARAMS,
-        )(place, tile_cols, row_counts, tiles, start_col, scale_col)
+        )(place, tile_cols, row_counts, tiles, u)
     )
     chunks = pair.astype(bf16).reshape(groups, share, width)
     product = exchange(exchange(chunks, GX), Z).astype(f32).sum(axis=0)
-    u_seg = lax.dynamic_slice_in_dim(start_col, line * share, share, 0).astype(f32)
-    u_seg = (scale_seg[:, None] * u_seg).astype(bf16).astype(f32)
-    w1 = scale_seg[:, None] * (product + u_seg)
+    w1 = scale_seg[:, None] * (product + u_seg.astype(f32))
     squares1 = jnp.sum(w1 * w1, axis=0)
 
     v_seg = (scale_seg[:, None] * w1).astype(bf16)

time: 220 us -> 176 us (0.80)
  blocking collectives: 103 us -> 80 us
  waiting for transfers between devices: 49.9 us -> 36.3 us
  starting transfers between devices: 53.4 us -> 46.9 us
    all_to_all x4 -> x6, blocking collectives: 103 us -> 80 us  [exchange(): return lax.all_to_all(array, axis, 0, 0, tiled=True)]
    all_to_all x4 -> x3, starting transfers between devices: 37.2 us -> 22 us  [exchange(): return lax.all_to_all(array, axis, 0, 0, tiled=True)]
    all_to_all x4 -> x3, waiting for transfers between devices: 46.9 us -> 32.5 us  [exchange(): return lax.all_to_all(array, axis, 0, 0, tiled=True)]
    ppermute x3, starting transfers between devices: 16.2 us -> 24.9 us  [swapped(): return lax.ppermute(array, CORE, [(0, 1), (1, 0)])]
  transfers between devices with their start and end apart: 7 -> 6, of which waited for: 6 -> 6; matrix products, arithmetic and copies ran while one was open for 0% -> 0% of each run, Pallas kernels for 0% -> 0%
where the time goes in v2:
time: 176 us; the launch traced here: 175 us
  blocking collectives  80 us (45%)
  starting transfers between devices  46.9 us (27%)
  waiting for transfers between devices  36.3 us (21%)
  Pallas kernels  4.25 us (2%)
  local copies, waits for them, and re-layouts  3.93 us (2%)
  other arithmetic  2.79 us (2%)
    all_to_all x6, blocking collectives, exchange(): return lax.all_to_all(array, axis, 0, 0, tiled=True)  80 us
    all_to_all x3, waiting for transfers between devices, exchange(): return lax.all_to_all(array, axis, 0, 0, tiled=True)  32.5 us
    ppermute x3, starting transfers between devices, swapped(): return lax.ppermute(array, CORE, [(0, 1), (1, 0)])  24.9 us
    all_to_all x3, starting transfers between devices, exchange(): return lax.all_to_all(array, axis, 0, 0, tiled=True)  22 us
    ppermute x3, waiting for transfers between devices, swapped(): return lax.ppermute(array, CORE, [(0, 1), (1, 0)])  3.79 us
  transfers between devices with their start and end apart: 6, of which 6 were waited for; matrix products, arithmetic and copies ran while one was open for 0% of the time, Pallas kernels for 0%

profile of v2, /device:TPU:1, one launch (start us, length us, event | category | flops | bytes accessed | tf_op | source)
XLA Modules:
  0.0 175.1 jit_solution(9587256064374158190)
XLA Ops:
  0.6 0.8 copy.31.counts
  1.4 1.4 copy-done.1
  2.8 1.3 shard_map.59
  4.2 8.9 %collective-permute-start = (f32[16,128]{1,0:T(8,128)S(1)}, f32[16,128]{1,0:T(8,128)S(1)}, u32[]{:S(2)}, u32[]{:S(2)}) collective-permute-start(f32[16,128]{1,0:T(8,128)S(1)} %shard_map.59), channel_id=1, source_target_pairs={{0,1},{1,0},{2,3},{3,2},{4,5},{5,4},{6,7},{7,6},{8,9},{9,8},{10,11... | collective-permute-start | bytes 24584 | tf_op jit(solution)/shard_map/ppermute | solution.py:107
  13.1 0.8 collective-permute-done
  14.0 11.6 %all_to_all.45 = bf16[16,80,128]{2,1,0:T(8,128)(2,1)S(1)} all-to-all(bf16[16,80,128]{2,1,0:T(8,128)(2,1)S(1)} %fusion.1), channel_id=1, replica_groups=mesh['gx_0'=4,'gx_1'=4,'gy_0'=16,'gy_1'=2] {'gx_0','gx_1'}, dimensions={0} | all-to-all | bytes 655360 | tf_op jit(solution)/shard_map/all_to_all | solution.py:18
  25.6 0.6 copy.33
  26.2 13.4 %all-to-all-start.1 = ((f32[16,2,128]{2,1,0:T(2,128)}), f32[16,2,128]{2,1,0:T(2,128)S(1)}, u32[]{:S(2)}, u32[]{:S(2)}) async-start(f32[16,2,128]{2,1,0:T(2,128)} %copy.33), calls=%async_computation.1 | async-start | bytes 32768 | tf_op jit(solution)/shard_map/all_to_all | solution.py:18
  39.6 11.4 %all-to-all-done.1 = f32[16,2,128]{2,1,0:T(2,128)S(1)} async-done(((f32[16,2,128]{2,1,0:T(2,128)}), f32[16,2,128]{2,1,0:T(2,128)S(1)}, u32[]{:S(2)}, u32[]{:S(2)}) %all-to-all-start.1) | async-done | bytes 16416 | tf_op jit(solution)/shard_map/all_to_all | solution.py:18
  51.2 0.7 broadcast_in_dim.16
  51.9 3.5 %all-to-all-start.2 = ((bf16[16,64,128]{2,1,0:T(8,128)(2,1)}), bf16[16,64,128]{2,1,0:T(8,128)(2,1)S(1)}, u32[]{:S(2)}, u32[]{:S(2)}) async-start(bf16[16,64,128]{2,1,0:T(8,128)(2,1)} %broadcast_in_dim.16), calls=%async_computation.2 | async-start | bytes 524288 | tf_op jit(solution)/shard_map/all_to_all | solution.py:18
  55.5 0.1 copy.36.cols
  55.6 7.3 %all-to-all-done.2 = bf16[16,64,128]{2,1,0:T(8,128)(2,1)S(1)} async-done(((bf16[16,64,128]{2,1,0:T(8,128)(2,1)}), bf16[16,64,128]{2,1,0:T(8,128)(2,1)S(1)}, u32[]{:S(2)}, u32[]{:S(2)}) %all-to-all-start.2) | async-done | bytes 262176 | tf_op jit(solution)/shard_map/all_to_all | solution.py:18
  63.0 1.4 shard_map.60
  64.4 6.0 %collective-permute-start.1 = (f32[1024,128]{1,0:T(8,128)S(1)}, f32[1024,128]{1,0:T(8,128)S(1)}, u32[]{:S(2)}, u32[]{:S(2)}) collective-permute-start(f32[1024,128]{1,0:T(8,128)S(1)} %get-tuple-element.7), channel_id=1, source_target_pairs={{0,1},{1,0},{2,3},{3,2},{4,5},{5,4},{6,7},{7,6},{8,9},{9,8},{10,11... | collective-permute-start | bytes 1572872 | tf_op jit(solution)/shard_map/ppermute | solution.py:107
  70.4 1.5 collective-permute-done.1
  71.9 10.7 %all_to_all.46 = bf16[16,64,128]{2,1,0:T(8,128)(2,1)S(1)} all-to-all(bf16[16,64,128]{2,1,0:T(8,128)(2,1)S(1)} %bitcast.44), channel_id=1, replica_groups=mesh['gx_0'=4,'gx_1'=4,'gy_0'=16,'gy_1'=2] {'gx_0','gx_1'}, dimensions={0} | all-to-all | bytes 524288 | tf_op jit(solution)/shard_map/all_to_all | solution.py:18
  82.7 15.4 %all_to_all.47 = bf16[16,64,128]{2,1,0:T(8,128)(2,1)S(1)} all-to-all(bf16[16,64,128]{2,1,0:T(8,128)(2,1)S(1)} %all_to_all.46), channel_id=1, replica_groups=mesh['gx_0'=4,'gx_1'=4,'gy_0'=16,'gy_1'=2] {'gy_0'}, dimensions={0} | all-to-all | bytes 524288 | tf_op jit(solution)/shard_map/all_to_all | solution.py:18
  98.1 0.1 fusion.8
  98.3 10.1 %all_to_all.48 = bf16[16,64,128]{2,1,0:T(8,128)(2,1)S(1)} all-to-all(bf16[16,64,128]{2,1,0:T(8,128)(2,1)S(1)} %broadcast_in_dim.18), channel_id=1, replica_groups=mesh['gx_0'=4,'gx_1'=4,'gy_0'=16,'gy_1'=2] {'gx_0','gx_1'}, dimensions={0} | all-to-all | bytes 524288 | tf_op jit(solution)/shard_map/all_to_all | solution.py:18
  108.4 1.6 shard_map.61
  109.9 10.0 %collective-permute-start.2 = (f32[1024,128]{1,0:T(8,128)S(1)}, f32[1024,128]{1,0:T(8,128)S(1)}, u32[]{:S(2)}, u32[]{:S(2)}) collective-permute-start(f32[1024,128]{1,0:T(8,128)S(1)} %get-tuple-element.9), channel_id=1, source_target_pairs={{0,1},{1,0},{2,3},{3,2},{4,5},{5,4},{6,7},{7,6},{8,9},{9,8},{10,11... | collective-permute-start | bytes 1572872 | tf_op jit(solution)/shard_map/ppermute | solution.py:107
  120.0 1.5 collective-permute-done.2
  121.5 0.7 add_convert_fusion
  122.3 5.0 %all-to-all-start.6 = ((bf16[16,64,128]{2,1,0:T(8,128)(2,1)}), bf16[16,64,128]{2,1,0:T(8,128)(2,1)S(1)}, u32[]{:S(2)}, u32[]{:S(2)}) async-start(bf16[16,64,128]{2,1,0:T(8,128)(2,1)} %bitcast.15), calls=%async_computation.6 | async-start | bytes 524288 | tf_op jit(solution)/shard_map/all_to_all | solution.py:18
  127.4 0.1 multiply_reduce_fusion.1
  127.5 13.8 %all-to-all-done.6 = bf16[16,64,128]{2,1,0:T(8,128)(2,1)S(1)} async-done(((bf16[16,64,128]{2,1,0:T(8,128)(2,1)}), bf16[16,64,128]{2,1,0:T(8,128)(2,1)S(1)}, u32[]{:S(2)}, u32[]{:S(2)}) %all-to-all-start.6) | async-done | bytes 262176 | tf_op jit(solution)/shard_map/all_to_all | solution.py:18
  141.4 0.1 multiply_reduce_fusion
  141.5 15.4 %all_to_all.49 = f32[32,2,128]{2,1,0:T(2,128)S(1)} all-to-all(f32[32,2,128]{2,1,0:T(2,128)S(1)} %broadcast_in_dim.19), channel_id=1, replica_groups=mesh['gx_0'=4,'gx_1'=4,'gy_0'=16,'gy_1'=2] {'gx_0','gx_1','gy_1'}, dimensions={0} | all-to-all | bytes 65536 | tf_op jit(solution)/shard_map/all_to_all | solution.py:18
  156.9 16.8 %all_to_all.50 = f32[16,2,128]{2,1,0:T(2,128)S(1)} all-to-all(f32[16,2,128]{2,1,0:T(2,128)S(1)} %broadcast_in_dim.20), channel_id=1, replica_groups=mesh['gx_0'=4,'gx_1'=4,'gy_0'=16,'gy_1'=2] {'gy_0'}, dimensions={0} | all-to-all | bytes 32768 | tf_op jit(solution)/shard_map/all_to_all | solution.py:18
  173.8 0.7 divide_convert_fusion
  174.5 0.6 pad_maximum_fusion.3
  (34 shorter events, 0.8 us)
Async XLA Ops:
  0.6 12.5 %copy-start = (bf16[2048,128]{1,0:T(8,128)(2,1)S(1)}, bf16[2048,128]{1,0:T(8,128)(2,1)}, u32[]{:S(2)}) copy-start(bf16[2048,128]{1,0:T(8,128)(2,1)} %param.7) | copy-start | bytes 1572868
  1.4 1.4 copy-start.1
  4.1 51.3 %copy-start.3 = (s32[16,3]{0,1:T(4,128)S(1)}, s32[16,3]{0,1:T(4,128)}, u32[]{:S(2)}) copy-start(s32[16,3]{0,1:T(4,128)} %param.5) | copy-start | bytes 580
  4.2 58.8 %copy-start.2 = (bf16[16,3,128,128]{3,2,1,0:T(8,128)(2,1)S(1)}, bf16[16,3,128,128]{3,2,1,0:T(8,128)(2,1)}, u32[]{:S(2)}) copy-start(bf16[16,3,128,128]{3,2,1,0:T(8,128)(2,1)} %tiles.5) | copy-start | bytes 4718596
  4.2 9.7 %collective-permute-start = (f32[16,128]{1,0:T(8,128)S(1)}, f32[16,128]{1,0:T(8,128)S(1)}, u32[]{:S(2)}, u32[]{:S(2)}) collective-permute-start(f32[16,128]{1,0:T(8,128)S(1)} %shard_map.59), channel_id=1, source_target_pairs={{0,1},{1,0},{2,3},{3,2},{4,5},{5,4},{6,7},{7,6},{8,9},{9,8},{10,11... | collective-permute-start | bytes 24584 | tf_op jit(solution)/shard_map/ppermute | solution.py:107
  26.2 24.8 %all-to-all-start.1 = ((f32[16,2,128]{2,1,0:T(2,128)}), f32[16,2,128]{2,1,0:T(2,128)S(1)}, u32[]{:S(2)}, u32[]{:S(2)}) async-start(f32[16,2,128]{2,1,0:T(2,128)} %copy.33), calls=%async_computation.1 | async-start | bytes 32768 | tf_op jit(solution)/shard_map/all_to_all | solution.py:18
  51.9 11.0 %all-to-all-start.2 = ((bf16[16,64,128]{2,1,0:T(8,128)(2,1)}), bf16[16,64,128]{2,1,0:T(8,128)(2,1)S(1)}, u32[]{:S(2)}, u32[]{:S(2)}) async-start(bf16[16,64,128]{2,1,0:T(8,128)(2,1)} %broadcast_in_dim.16), calls=%async_computation.2 | async-start | bytes 524288 | tf_op jit(solution)/shard_map/all_to_all | solution.py:18
  64.4 7.5 %collective-permute-start.1 = (f32[1024,128]{1,0:T(8,128)S(1)}, f32[1024,128]{1,0:T(8,128)S(1)}, u32[]{:S(2)}, u32[]{:S(2)}) collective-permute-start(f32[1024,128]{1,0:T(8,128)S(1)} %get-tuple-element.7), channel_id=1, source_target_pairs={{0,1},{1,0},{2,3},{3,2},{4,5},{5,4},{6,7},{7,6},{8,9},{9,8},{10,11... | collective-permute-start | bytes 1572872 | tf_op jit(solution)/shard_map/ppermute | solution.py:107
  109.9 11.6 %collective-permute-start.2 = (f32[1024,128]{1,0:T(8,128)S(1)}, f32[1024,128]{1,0:T(8,128)S(1)}, u32[]{:S(2)}, u32[]{:S(2)}) collective-permute-start(f32[1024,128]{1,0:T(8,128)S(1)} %get-tuple-element.9), channel_id=1, source_target_pairs={{0,1},{1,0},{2,3},{3,2},{4,5},{5,4},{6,7},{7,6},{8,9},{9,8},{10,11... | collective-permute-start | bytes 1572872 | tf_op jit(solution)/shard_map/ppermute | solution.py:107
  122.3 19.1 %all-to-all-start.6 = ((bf16[16,64,128]{2,1,0:T(8,128)(2,1)}), bf16[16,64,128]{2,1,0:T(8,128)(2,1)S(1)}, u32[]{:S(2)}, u32[]{:S(2)}) async-start(bf16[16,64,128]{2,1,0:T(8,128)(2,1)} %bitcast.15), calls=%async_computation.6 | async-start | bytes 524288 | tf_op jit(solution)/shard_map/all_to_all | solution.py:18

commit v3 on v2

--- a/solution.py
+++ b/solution.py
@@ -24,23 +24,27 @@
 
 
 def row_sum_kernel(counts, tiles, out):
-    row_tiles, slots, side, _ = tiles.shape
-    for r in range(row_tiles):
+    here, slots, side, _ = tiles.shape
+    step = pl.program_id(0)
+    slot = lax.broadcasted_iota(jnp.int32, (8, slots * side), 1) // side
+    for r in range(here):
         wide = jnp.concatenate([tiles[r, s] for s in range(slots)], axis=1)
-        slot = lax.broadcasted_iota(jnp.int32, (8, slots * side), 1) // side
-        live = jnp.where(slot < counts[r, 0], 1.0, 0.0).astype(tiles.dtype)
+        which = lax.broadcasted_iota(jnp.int32, counts.shape, 1) == step * here + r
+        count = jnp.sum(jnp.where(which, counts[...], 0), axis=1, keepdims=True)
+        live = jnp.where(slot < count, 1.0, 0.0).astype(tiles.dtype)
         sums = lax.dot_general(
             live, wide, (((1,), (1,)), ((), ())), preferred_element_type=jnp.float32
         )
-        out[r : r + 1] = sums[0:1]
+        out[pl.ds(step * here + r, 1)] = sums[0:1]
 
 
 def pick(cols, counts, column, r, slots, side):
     parts = []
     for s in range(slots):
-        start = pl.multiple_of(cols[r, s] * side, side)
+        start = pl.multiple_of(cols[s, r] * side, side)
         part = column[pl.ds(start, side), :]
-        parts.append(jnp.where(s < counts[r, 0], part, jnp.zeros_like(part)))
+        live = s < counts[0, r]
+        parts.append(jnp.where(live, part, jnp.zeros_like(part)))
     return jnp.concatenate(parts, axis=0)
 
 
@@ -95,34 +99,44 @@
     f32, bf16 = jnp.float32, jnp.bfloat16
 
     place = jnp.stack([core, line, plane]).astype(jnp.int32)
+    cols = tile_cols.T
+    counts = row_counts.T
+    steps = 2
     row_sums = pl.pallas_call(
         row_sum_kernel,
+        grid=(steps,),
         out_shape=jax.ShapeDtypeStruct((row_tiles, side), f32),
-        in_specs=[SMEM, VMEM],
-        out_specs=VMEM,
-        compiler_params=PARAMS,
-    )(row_counts, tiles)
+        in_specs=[
+            pl.BlockSpec((1, row_tiles), lambda g: (0, 0)),
+            pl.BlockSpec(
+                (row_tiles // steps, slot_count, side, side), lambda g: (g, 0, 0, 0)
+            ),
+        ],
+        out_specs=pl.BlockSpec((row_tiles, side), lambda g: (0, 0)),
+    )(counts, tiles)
 
     def swapped(array):
         return lax.ppermute(array, CORE, [(0, 1), (1, 0)])
 
-    row_sums = row_sums + swapped(row_sums)
     start_half = lax.dynamic_slice_in_dim(start_block, core * half_rows, half_rows, 0)
-    part = lax.dynamic_slice_in_dim(row_sums, core * half_tiles, half_tiles, 0)
-    part = jnp.repeat(part, 2, axis=0)
+    part = row_sums.reshape(2, groups, share).transpose(1, 0, 2).reshape(groups, side)
     high = lax.reduce_precision(part, 8, 7)
     middle = lax.reduce_precision(part - high, 8, 7)
     terms = jnp.stack([high, middle, part - high - middle], axis=1).astype(bf16)
     terms = jnp.pad(terms, ((0, 0), (0, 13), (0, 0)))
     sent = [start_half.reshape(groups, share, width), terms]
-    got = exchange(jnp.concatenate(sent, axis=1), GX)
+    sent = jnp.concatenate(sent, axis=1)
+    sent, place = lax.optimization_barrier((sent, place))
+    got = exchange(sent, GX)
     start_seg = lax.dynamic_index_in_dim(got, plane, 0, keepdims=False)[:share]
     part = got[:, share : share + 3].astype(f32).sum(axis=1)
 
-    degree = 1.0 + exchange(jnp.stack([part, row_sums], axis=1), Z).sum(axis=0)
+    both = jnp.concatenate([part[:, None], row_sums[:, None]], axis=2)
+    both = jnp.repeat(both, 2, axis=0)
+    degree = 1.0 + exchange(both, GY).sum(axis=(0, 1))
     scale = 1.0 / jnp.sqrt(degree)
-    scale_seg = lax.dynamic_slice_in_dim(scale[0], line % 2 * share, share, 0)
-    scale_own = lax.dynamic_slice_in_dim(scale[1], core * share, share, 0)
+    scale_seg = lax.dynamic_slice_in_dim(scale, core * share, share, 0)
+    scale_own = lax.dynamic_slice_in_dim(scale, side + core * share, share, 0)
 
     halves = [jax.ShapeDtypeStruct((half_rows, width), f32)] * 2
 
@@ -138,7 +152,7 @@
             in_specs=[SMEM] * 3 + [VMEM] * 2,
             out_specs=[VMEM] * 2,
             compiler_params=PARAMS,
-        )(place, tile_cols, row_counts, tiles, u)
+        )(place, cols, counts, tiles, u)
     )
     chunks = pair.astype(bf16).reshape(groups, share, width)
     product = exchange(exchange(chunks, GX), Z).astype(f32).sum(axis=0)
@@ -146,6 +160,7 @@
     squares1 = jnp.sum(w1 * w1, axis=0)
 
     v_seg = (scale_seg[:, None] * w1).astype(bf16)
+    v_seg, squares1, scale_own = lax.optimization_barrier((v_seg, squares1, scale_own))
     v = from_everyone(v_seg, GX).reshape(half_rows, width)
     pair = pair_sum(
         *pl.pallas_call(
@@ -154,7 +169,7 @@
             in_specs=[SMEM] * 3 + [VMEM] * 2,
             out_specs=[VMEM] * 2,
             compiler_params=PARAMS,
-        )(place, tile_cols, row_counts, tiles, v)
+        )(place, cols, counts, tiles, v)
     ).reshape(row_tiles, share, width)
     product = exchange(pair.astype(bf16), Z).astype(f32).sum(axis=0)
     w2 = scale_own[:, None] * product

time: 176 us -> 171 us (0.972)
  blocking collectives: 80 us -> 113 us
  waiting for transfers between devices: 36.3 us -> 15.1 us
  starting transfers between devices: 46.9 us -> 32.1 us
  local copies, waits for them, and re-layouts: 3.93 us -> 1.9 us
    all_to_all x6 -> x8, blocking collectives: 80 us -> 113 us  [exchange(): return lax.all_to_all(array, axis, 0, 0, tiled=True)]
    all_to_all x3 -> x1, waiting for transfers between devices: 32.5 us -> 12.1 us  [exchange(): return lax.all_to_all(array, axis, 0, 0, tiled=True)]
    ppermute x3 -> x2, starting transfers between devices: 24.9 us -> 14.4 us  [swapped(): return lax.ppermute(array, CORE, [(0, 1), (1, 0)])]
    all_to_all x3 -> x1, starting transfers between devices: 22 us -> 17.6 us  [exchange(): return lax.all_to_all(array, axis, 0, 0, tiled=True)]
    unnamed x11, local copies, waits for them, and re-layouts: 2.31 us -> 0.03 us
    ppermute x3 -> x2, waiting for transfers between devices: 3.79 us -> 3.03 us  [swapped(): return lax.ppermute(array, CORE, [(0, 1), (1, 0)])]
  transfers between devices with their start and end apart: 6 -> 3, of which waited for: 6 -> 3; matrix products, arithmetic and copies ran while one was open for 0% -> 0% of each run, Pallas kernels for 0% -> 0%
where the time goes in v3:
time: 171 us; the launch traced here: 170 us
  blocking collectives  113 us (66%)
  starting transfers between devices  32.1 us (19%)
  waiting for transfers between devices  15.1 us (9%)
  Pallas kernels  5.17 us (3%)
  other arithmetic  2.1 us (1%)
  local copies, waits for them, and re-layouts  1.9 us (1%)
    all_to_all x8, blocking collectives, exchange(): return lax.all_to_all(array, axis, 0, 0, tiled=True)  113 us
    all_to_all x1, starting transfers between devices, exchange(): return lax.all_to_all(array, axis, 0, 0, tiled=True)  17.6 us
    ppermute x2, starting transfers between devices, swapped(): return lax.ppermute(array, CORE, [(0, 1), (1, 0)])  14.4 us
    all_to_all x1, waiting for transfers between devices, exchange(): return lax.all_to_all(array, axis, 0, 0, tiled=True)  12.1 us
  transfers between devices with their start and end apart: 3, of which 3 were waited for; matrix products, arithmetic and copies ran while one was open for 0% of the time, Pallas kernels for 0%

profile of v3, /device:TPU:1, one launch (start us, length us, event | category | flops | bytes accessed | tf_op | source)
XLA Modules:
  0.0 170.0 jit_solution(6814292166511286257)
XLA Ops:
  0.6 0.0 copy-start
  0.7 2.7 %shard_map.59 = f32[16,128]{1,0:T(8,128)} custom-call(s32[1,16]{1,0:T(1,128)} %bitcast.37, bf16[16,3,128,128]{3,2,1,0:T(8,128)(2,1)} %tiles.5), custom_call_target="tpu_custom_call" | custom-call | tf_op jit(solution)/shard_map/pallas_call | solution.py:105
  3.3 0.9 reshape.78
  4.2 0.1 reshape.79
  4.4 0.1 pad_add_fusion.place
  4.5 15.3 %all_to_all.45 = bf16[16,80,128]{2,1,0:T(8,128)(2,1)S(1)} all-to-all(bf16[16,80,128]{2,1,0:T(8,128)(2,1)S(1)} %fusion.1), channel_id=1, replica_groups=mesh['gx_0'=4,'gx_1'=4,'gy_0'=16,'gy_1'=2] {'gx_0','gx_1'}, dimensions={0} | all-to-all | bytes 655360 | tf_op jit(solution)/shard_map/all_to_all | solution.py:18
  19.9 0.0 copy-done.4
  19.9 0.7 broadcast_in_dim.21
  20.6 17.6 %all-to-all-start.1 = ((f32[32,1,256]{2,1,0:T(1,128)}), f32[32,1,256]{2,1,0:T(1,128)S(1)}, u32[]{:S(2)}, u32[]{:S(2)}) async-start(f32[32,1,256]{2,1,0:T(1,128)} %broadcast_in_dim.21), calls=%async_computation.1 | async-start | bytes 65536 | tf_op jit(solution)/shard_map/all_to_all | solution.py:18
  38.2 12.1 %all-to-all-done.1 = f32[32,1,256]{2,1,0:T(1,128)S(1)} async-done(((f32[32,1,256]{2,1,0:T(1,128)}), f32[32,1,256]{2,1,0:T(1,128)S(1)}, u32[]{:S(2)}, u32[]{:S(2)}) %all-to-all-start.1) | async-done | bytes 32800 | tf_op jit(solution)/shard_map/all_to_all | solution.py:18
  50.3 0.1 reduce_sum.73
  50.4 0.1 fusion.7
  50.5 0.1 fusion.5
  50.6 10.2 %all_to_all.46 = bf16[16,64,128]{2,1,0:T(8,128)(2,1)S(1)} all-to-all(bf16[16,64,128]{2,1,0:T(8,128)(2,1)S(1)} %broadcast_in_dim.23), channel_id=1, replica_groups=mesh['gx_0'=4,'gx_1'=4,'gy_0'=16,'gy_1'=2] {'gx_0','gx_1'}, dimensions={0} | all-to-all | bytes 524288 | tf_op jit(solution)/shard_map/all_to_all | solution.py:18
  60.8 1.2 shard_map.60
  62.0 4.4 %collective-permute-start = (f32[1024,128]{1,0:T(8,128)S(1)}, f32[1024,128]{1,0:T(8,128)S(1)}, u32[]{:S(2)}, u32[]{:S(2)}) collective-permute-start(f32[1024,128]{1,0:T(8,128)S(1)} %get-tuple-element.14), channel_id=1, source_target_pairs={{0,1},{1,0},{2,3},{3,2},{4,5},{5,4},{6,7},{7,6},{8,9},{9,8},{10,11... | collective-permute-start | bytes 1572872 | tf_op jit(solution)/shard_map/ppermute | solution.py:119
  66.4 1.5 collective-permute-done
  67.9 0.1 add_convert_fusion.1
  68.0 10.7 %all_to_all.47 = bf16[16,64,128]{2,1,0:T(8,128)(2,1)S(1)} all-to-all(bf16[16,64,128]{2,1,0:T(8,128)(2,1)S(1)} %bitcast.41), channel_id=1, replica_groups=mesh['gx_0'=4,'gx_1'=4,'gy_0'=16,'gy_1'=2] {'gx_0','gx_1'}, dimensions={0} | all-to-all | bytes 524288 | tf_op jit(solution)/shard_map/all_to_all | solution.py:18
  78.7 15.4 %all_to_all.48 = bf16[16,64,128]{2,1,0:T(8,128)(2,1)S(1)} all-to-all(bf16[16,64,128]{2,1,0:T(8,128)(2,1)S(1)} %all_to_all.47), channel_id=1, replica_groups=mesh['gx_0'=4,'gx_1'=4,'gy_0'=16,'gy_1'=2] {'gy_0'}, dimensions={0} | all-to-all | bytes 524288 | tf_op jit(solution)/shard_map/all_to_all | solution.py:18
  94.2 0.1 multiply_reduce_fusion.1
  94.3 10.1 %all_to_all.49 = bf16[16,64,128]{2,1,0:T(8,128)(2,1)S(1)} all-to-all(bf16[16,64,128]{2,1,0:T(8,128)(2,1)S(1)} %broadcast_in_dim.48), channel_id=1, replica_groups=mesh['gx_0'=4,'gx_1'=4,'gy_0'=16,'gy_1'=2] {'gx_0','gx_1'}, dimensions={0} | all-to-all | bytes 524288 | tf_op jit(solution)/shard_map/all_to_all | solution.py:18
  104.5 1.3 shard_map.61
  105.8 10.0 %collective-permute-start.1 = (f32[1024,128]{1,0:T(8,128)S(1)}, f32[1024,128]{1,0:T(8,128)S(1)}, u32[]{:S(2)}, u32[]{:S(2)}) collective-permute-start(f32[1024,128]{1,0:T(8,128)S(1)} %get-tuple-element.18), channel_id=1, source_target_pairs={{0,1},{1,0},{2,3},{3,2},{4,5},{5,4},{6,7},{7,6},{8,9},{9,8},{10,11... | collective-permute-start | bytes 1572872 | tf_op jit(solution)/shard_map/ppermute | solution.py:119
  115.8 1.5 collective-permute-done.1
  117.3 0.1 add_convert_fusion
  117.4 18.9 %all_to_all.50 = bf16[16,64,128]{2,1,0:T(8,128)(2,1)S(1)} all-to-all(bf16[16,64,128]{2,1,0:T(8,128)(2,1)S(1)} %bitcast.42), channel_id=1, replica_groups=mesh['gx_0'=4,'gx_1'=4,'gy_0'=16,'gy_1'=2] {'gy_0'}, dimensions={0} | all-to-all | bytes 524288 | tf_op jit(solution)/shard_map/all_to_all | solution.py:18
  136.3 0.1 multiply_reduce_fusion
  136.4 15.4 %all_to_all.51 = f32[32,2,128]{2,1,0:T(2,128)S(1)} all-to-all(f32[32,2,128]{2,1,0:T(2,128)S(1)} %broadcast_in_dim.49), channel_id=1, replica_groups=mesh['gx_0'=4,'gx_1'=4,'gy_0'=16,'gy_1'=2] {'gx_0','gx_1','gy_1'}, dimensions={0} | all-to-all | bytes 65536 | tf_op jit(solution)/shard_map/all_to_all | solution.py:18
  151.8 16.8 %all_to_all.52 = f32[16,2,128]{2,1,0:T(2,128)S(1)} all-to-all(f32[16,2,128]{2,1,0:T(2,128)S(1)} %broadcast_in_dim.50), channel_id=1, replica_groups=mesh['gx_0'=4,'gx_1'=4,'gy_0'=16,'gy_1'=2] {'gy_0'}, dimensions={0} | all-to-all | bytes 32768 | tf_op jit(solution)/shard_map/all_to_all | solution.py:18
  168.7 0.7 divide_convert_fusion
  169.4 0.6 pad_maximum_fusion.2
  (28 shorter events, 0.5 us)
Async XLA Ops:
  0.6 3.7 %copy-start = (bf16[2048,128]{1,0:T(8,128)(2,1)S(1)}, bf16[2048,128]{1,0:T(8,128)(2,1)}, u32[]{:S(2)}) copy-start(bf16[2048,128]{1,0:T(8,128)(2,1)} %param.7) | copy-start | bytes 1572868
  3.3 16.5 %copy-start.4 = (f32[16,128]{1,0:T(8,128)S(1)}, f32[16,128]{1,0:T(8,128)}, u32[]{:S(2)}) copy-start(f32[16,128]{1,0:T(8,128)} %shard_map.59) | copy-start | bytes 24580
  3.3 57.5 %copy-start.1 = (bf16[16,3,128,128]{3,2,1,0:T(8,128)(2,1)S(1)}, bf16[16,3,128,128]{3,2,1,0:T(8,128)(2,1)}, u32[]{:S(2)}) copy-start(bf16[16,3,128,128]{3,2,1,0:T(8,128)(2,1)} %tiles.5) | copy-start | bytes 4718596
  3.3 57.5 %copy-start.2 = (s32[16,3]{0,1:T(4,128)S(1)}, s32[16,3]{0,1:T(4,128)}, u32[]{:S(2)}) copy-start(s32[16,3]{0,1:T(4,128)} %param.5) | copy-start | bytes 580
  3.3 57.5 %copy-start.3 = (s32[16,1]{0,1:T(1,128)S(1)}, s32[16,1]{0,1:T(1,128)}, u32[]{:S(2)}) copy-start(s32[16,1]{0,1:T(1,128)} %param.6) | copy-start | bytes 196
  20.6 29.8 %all-to-all-start.1 = ((f32[32,1,256]{2,1,0:T(1,128)}), f32[32,1,256]{2,1,0:T(1,128)S(1)}, u32[]{:S(2)}, u32[]{:S(2)}) async-start(f32[32,1,256]{2,1,0:T(1,128)} %broadcast_in_dim.21), calls=%async_computation.1 | async-start | bytes 65536 | tf_op jit(solution)/shard_map/all_to_all | solution.py:18
  62.0 5.9 %collective-permute-start = (f32[1024,128]{1,0:T(8,128)S(1)}, f32[1024,128]{1,0:T(8,128)S(1)}, u32[]{:S(2)}, u32[]{:S(2)}) collective-permute-start(f32[1024,128]{1,0:T(8,128)S(1)} %get-tuple-element.14), channel_id=1, source_target_pairs={{0,1},{1,0},{2,3},{3,2},{4,5},{5,4},{6,7},{7,6},{8,9},{9,8},{10,11... | collective-permute-start | bytes 1572872 | tf_op jit(solution)/shard_map/ppermute | solution.py:119
  105.8 11.6 %collective-permute-start.1 = (f32[1024,128]{1,0:T(8,128)S(1)}, f32[1024,128]{1,0:T(8,128)S(1)}, u32[]{:S(2)}, u32[]{:S(2)}) collective-permute-start(f32[1024,128]{1,0:T(8,128)S(1)} %get-tuple-element.18), channel_id=1, source_target_pairs={{0,1},{1,0},{2,3},{3,2},{4,5},{5,4},{6,7},{7,6},{8,9},{9,8},{10,11... | collective-permute-start | bytes 1572872 | tf_op jit(solution)/shard_map/ppermute | solution.py:119

commit v4 on v3

--- a/solution.py
+++ b/solution.py
@@ -23,19 +23,37 @@
     return exchange(jnp.broadcast_to(array[None], (peers, *array.shape)), axis)
 
 
-def row_sum_kernel(counts, tiles, out):
+def row_sum_kernel(counts, tiles, out, terms, held):
     here, slots, side, _ = tiles.shape
-    step = pl.program_id(0)
+    half = pl.program_id(0)
     slot = lax.broadcasted_iota(jnp.int32, (8, slots * side), 1) // side
-    for r in range(here):
-        wide = jnp.concatenate([tiles[r, s] for s in range(slots)], axis=1)
-        which = lax.broadcasted_iota(jnp.int32, counts.shape, 1) == step * here + r
+    mine = lax.broadcasted_iota(jnp.int32, (1, side), 1) // (side // 2) == half
+    row = lax.broadcasted_iota(jnp.int32, terms.shape[1:], 0)
+    for t in range(here):
+        wide = jnp.concatenate([tiles[t, s] for s in range(slots)], axis=1)
+        which = lax.broadcasted_iota(jnp.int32, counts.shape, 1) == half * here + t
         count = jnp.sum(jnp.where(which, counts[...], 0), axis=1, keepdims=True)
         live = jnp.where(slot < count, 1.0, 0.0).astype(tiles.dtype)
         sums = lax.dot_general(
             live, wide, (((1,), (1,)), ((), ())), preferred_element_type=jnp.float32
-        )
-        out[pl.ds(step * here + r, 1)] = sums[0:1]
+        )[0:1]
+        out[pl.ds(half * here + t, 1)] = sums
+        turned = pltpu.roll(sums, side // 2, 1)
+        for part in range(2):
+            at = pl.ds(2 * t + part, 1)
+            held[at] = jnp.where(
+                mine, jnp.where(half == part, sums, turned), held[at]
+            )
+
+    @pl.when(half == 1)
+    def _():
+        for p in range(2 * here):
+            value = held[p : p + 1]
+            high = value.astype(terms.dtype).astype(jnp.float32)
+            middle = (value - high).astype(terms.dtype).astype(jnp.float32)
+            low = value - high - middle
+            block = jnp.where(row == 1, middle, jnp.where(row == 2, low, 0.0))
+            terms[p] = jnp.where(row == 0, high, block).astype(terms.dtype)
 
 
 def pick(cols, counts, column, r, slots, side):
@@ -59,7 +77,7 @@
                 wide,
                 pick(cols, counts, column, r, slots, side),
                 preferred_element_type=jnp.float32,
-            )
+            ).astype(out.dtype)
 
 
 def second_kernel(place, cols, counts, tiles, column, mine, other):
@@ -76,7 +94,7 @@
             own = column[pl.ds((r % half) * side + part * share, share), :]
             value = jnp.dot(wide, picked, preferred_element_type=jnp.float32)
             value = value + jnp.where(diagonal, own.astype(jnp.float32), 0.0)
-            out[r * share : (r + 1) * share, :] = value
+            out[r * share : (r + 1) * share, :] = value.astype(out.dtype)
 
 
 SMEM = pl.BlockSpec(memory_space=pltpu.SMEM)
@@ -102,31 +120,35 @@
     cols = tile_cols.T
     counts = row_counts.T
     steps = 2
-    row_sums = pl.pallas_call(
+    row_sums, terms = pl.pallas_call(
         row_sum_kernel,
         grid=(steps,),
-        out_shape=jax.ShapeDtypeStruct((row_tiles, side), f32),
+        out_shape=[
+            jax.ShapeDtypeStruct((row_tiles, side), f32),
+            jax.ShapeDtypeStruct((groups, 16, side), bf16),
+        ],
         in_specs=[
             pl.BlockSpec((1, row_tiles), lambda g: (0, 0)),
             pl.BlockSpec(
                 (row_tiles // steps, slot_count, side, side), lambda g: (g, 0, 0, 0)
             ),
         ],
-        out_specs=pl.BlockSpec((row_tiles, side), lambda g: (0, 0)),
+        out_specs=[
+            pl.BlockSpec((row_tiles, side), lambda g: (0, 0)),
+            pl.BlockSpec((groups, 16, side), lambda g: (0, 0, 0)),
+        ],
+        scratch_shapes=[pltpu.VMEM((groups, side), f32)],
     )(counts, tiles)
 
     def swapped(array):
         return lax.ppermute(array, CORE, [(0, 1), (1, 0)])
 
     start_half = lax.dynamic_slice_in_dim(start_block, core * half_rows, half_rows, 0)
-    part = row_sums.reshape(2, groups, share).transpose(1, 0, 2).reshape(groups, side)
-    high = lax.reduce_precision(part, 8, 7)
-    middle = lax.reduce_precision(part - high, 8, 7)
-    terms = jnp.stack([high, middle, part - high - middle], axis=1).astype(bf16)
-    terms = jnp.pad(terms, ((0, 0), (0, 13), (0, 0)))
     sent = [start_half.reshape(groups, share, width), terms]
     sent = jnp.concatenate(sent, axis=1)
-    sent, place = lax.optimization_barrier((sent, place))
+    at_seg = core * share
+    at_own = side + at_seg
+    sent, place, at_seg, at_own = lax.optimization_barrier((sent, place, at_seg, at_own))
     got = exchange(sent, GX)
     start_seg = lax.dynamic_index_in_dim(got, plane, 0, keepdims=False)[:share]
     part = got[:, share : share + 3].astype(f32).sum(axis=1)
@@ -135,13 +157,13 @@
     both = jnp.repeat(both, 2, axis=0)
     degree = 1.0 + exchange(both, GY).sum(axis=(0, 1))
     scale = 1.0 / jnp.sqrt(degree)
-    scale_seg = lax.dynamic_slice_in_dim(scale, core * share, share, 0)
-    scale_own = lax.dynamic_slice_in_dim(scale, side + core * share, share, 0)
-
-    halves = [jax.ShapeDtypeStruct((half_rows, width), f32)] * 2
+    scale_seg = lax.dynamic_slice_in_dim(scale, at_seg, share, 0)
+    scale_own = lax.dynamic_slice_in_dim(scale, at_own, share, 0)
+
+    halves = [jax.ShapeDtypeStruct((half_rows, width), t) for t in (f32, bf16)]
 
     def pair_sum(mine, other):
-        return mine + swapped(other)
+        return mine + swapped(other).astype(f32)
 
     u_seg = (scale_seg[:, None] * start_seg.astype(f32)).astype(bf16)
     u = from_everyone(u_seg, GX).reshape(half_rows, width)

time: 171 us -> 170 us (level)
  no operation moved by 1% of the time
where the time goes in v4:
time: 170 us; the launch traced here: 169 us
  blocking collectives  113 us (66%)
  starting transfers between devices  32.1 us (19%)
  waiting for transfers between devices  14.4 us (8%)
  Pallas kernels  5.36 us (3%)
  other arithmetic  3 us (2%)
    all_to_all x8, blocking collectives, exchange(): return lax.all_to_all(array, axis, 0, 0, tiled=True)  113 us
    all_to_all x1, starting transfers between devices, exchange(): return lax.all_to_all(array, axis, 0, 0, tiled=True)  17.6 us
    ppermute x2, starting transfers between devices, swapped(): return lax.ppermute(array, CORE, [(0, 1), (1, 0)])  14.4 us
    all_to_all x1, waiting for transfers between devices, exchange(): return lax.all_to_all(array, axis, 0, 0, tiled=True)  12.1 us
  transfers between devices with their start and end apart: 3, of which 3 were waited for; matrix products, arithmetic and copies ran while one was open for 0% of the time, Pallas kernels for 0%

profile of v4, /device:TPU:1, one launch (start us, length us, event | category | flops | bytes accessed | tf_op | source)
XLA Modules:
  0.0 169.4 jit_solution(1454248698391014808)
XLA Ops:
  0.6 0.0 copy-start
  0.7 2.9 %shard_map.59 = (f32[16,128]{1,0:T(8,128)}, bf16[16,16,128]{2,1,0:T(8,128)(2,1)}) custom-call(s32[1,16]{1,0:T(1,128)} %bitcast.34, bf16[16,3,128,128]{3,2,1,0:T(8,128)(2,1)} %tiles.5), custom_call_target="tpu_custom_call" | custom-call | tf_op jit(solution)/shard_map/pallas_call | solution.py:123
  3.5 0.0 copy-start.2
  3.5 0.0 copy-start.3
  3.6 1.0 pad_maximum_fusion
  4.6 0.1 pad_add_fusion.place
  4.6 15.3 %all_to_all.45 = bf16[16,80,128]{2,1,0:T(8,128)(2,1)S(1)} all-to-all(bf16[16,80,128]{2,1,0:T(8,128)(2,1)S(1)} %pad_maximum_fusion), channel_id=1, replica_groups=mesh['gx_0'=4,'gx_1'=4,'gy_0'=16,'gy_1'=2] {'gx_0','gx_1'}, dimensions={0} | all-to-all | bytes 655360 | tf_op jit(solution)/shard_map/all_to_all | solution.py:18
  20.0 0.7 broadcast_in_dim.21
  20.7 17.6 %all-to-all-start.1 = ((f32[32,1,256]{2,1,0:T(1,128)}), f32[32,1,256]{2,1,0:T(1,128)S(1)}, u32[]{:S(2)}, u32[]{:S(2)}) async-start(f32[32,1,256]{2,1,0:T(1,128)} %broadcast_in_dim.21), calls=%async_computation.1 | async-start | bytes 65536 | tf_op jit(solution)/shard_map/all_to_all | solution.py:18
  38.3 12.1 %all-to-all-done.1 = f32[32,1,256]{2,1,0:T(1,128)S(1)} async-done(((f32[32,1,256]{2,1,0:T(1,128)}), f32[32,1,256]{2,1,0:T(1,128)S(1)}, u32[]{:S(2)}, u32[]{:S(2)}) %all-to-all-start.1) | async-done | bytes 32800 | tf_op jit(solution)/shard_map/all_to_all | solution.py:18
  50.5 0.1 reduce_sum.73
  50.5 0.1 fusion.4
  50.6 0.1 fusion.3
  50.7 10.2 %all_to_all.46 = bf16[16,64,128]{2,1,0:T(8,128)(2,1)S(1)} all-to-all(bf16[16,64,128]{2,1,0:T(8,128)(2,1)S(1)} %broadcast_in_dim.23), channel_id=1, replica_groups=mesh['gx_0'=4,'gx_1'=4,'gy_0'=16,'gy_1'=2] {'gx_0','gx_1'}, dimensions={0} | all-to-all | bytes 524288 | tf_op jit(solution)/shard_map/all_to_all | solution.py:18
  61.0 1.2 shard_map.60
  62.2 4.4 %collective-permute-start = (bf16[1024,128]{1,0:T(8,128)(2,1)S(1)}, bf16[1024,128]{1,0:T(8,128)(2,1)S(1)}, u32[]{:S(2)}, u32[]{:S(2)}) collective-permute-start(bf16[1024,128]{1,0:T(8,128)(2,1)S(1)} %get-tuple-element.21), channel_id=1, source_target_pairs={{0,1},{1,0},{2,3},{3,2},{4,5},{5,4},{6,7},{7,6},{8,9},{9,8},{10,11... | collective-permute-start | bytes 786440 | tf_op jit(solution)/shard_map/ppermute | solution.py:144
  66.6 1.1 collective-permute-done
  67.7 0.1 add_convert_fusion.1
  67.8 10.7 %all_to_all.47 = bf16[16,64,128]{2,1,0:T(8,128)(2,1)S(1)} all-to-all(bf16[16,64,128]{2,1,0:T(8,128)(2,1)S(1)} %bitcast.38), channel_id=1, replica_groups=mesh['gx_0'=4,'gx_1'=4,'gy_0'=16,'gy_1'=2] {'gx_0','gx_1'}, dimensions={0} | all-to-all | bytes 524288 | tf_op jit(solution)/shard_map/all_to_all | solution.py:18
  78.5 15.4 %all_to_all.48 = bf16[16,64,128]{2,1,0:T(8,128)(2,1)S(1)} all-to-all(bf16[16,64,128]{2,1,0:T(8,128)(2,1)S(1)} %all_to_all.47), channel_id=1, replica_groups=mesh['gx_0'=4,'gx_1'=4,'gy_0'=16,'gy_1'=2] {'gy_0'}, dimensions={0} | all-to-all | bytes 524288 | tf_op jit(solution)/shard_map/all_to_all | solution.py:18
  93.9 0.1 multiply_reduce_fusion.1
  94.1 10.1 %all_to_all.49 = bf16[16,64,128]{2,1,0:T(8,128)(2,1)S(1)} all-to-all(bf16[16,64,128]{2,1,0:T(8,128)(2,1)S(1)} %broadcast_in_dim.48), channel_id=1, replica_groups=mesh['gx_0'=4,'gx_1'=4,'gy_0'=16,'gy_1'=2] {'gx_0','gx_1'}, dimensions={0} | all-to-all | bytes 524288 | tf_op jit(solution)/shard_map/all_to_all | solution.py:18
  104.2 1.3 shard_map.61
  105.5 10.0 %collective-permute-start.1 = (bf16[1024,128]{1,0:T(8,128)(2,1)S(1)}, bf16[1024,128]{1,0:T(8,128)(2,1)S(1)}, u32[]{:S(2)}, u32[]{:S(2)}) collective-permute-start(bf16[1024,128]{1,0:T(8,128)(2,1)S(1)} %get-tuple-element.26), channel_id=1, source_target_pairs={{0,1},{1,0},{2,3},{3,2},{4,5},{5,4},{6,7},{7,6},{8,9},{9,8},{10,11... | collective-permute-start | bytes 786440 | tf_op jit(solution)/shard_map/ppermute | solution.py:144
  115.6 1.1 collective-permute-done.1
  116.7 0.1 add_convert_fusion
  116.8 18.9 %all_to_all.50 = bf16[16,64,128]{2,1,0:T(8,128)(2,1)S(1)} all-to-all(bf16[16,64,128]{2,1,0:T(8,128)(2,1)S(1)} %bitcast.39), channel_id=1, replica_groups=mesh['gx_0'=4,'gx_1'=4,'gy_0'=16,'gy_1'=2] {'gy_0'}, dimensions={0} | all-to-all | bytes 524288 | tf_op jit(solution)/shard_map/all_to_all | solution.py:18
  135.7 0.1 multiply_reduce_fusion
  135.8 15.4 %all_to_all.51 = f32[32,2,128]{2,1,0:T(2,128)S(1)} all-to-all(f32[32,2,128]{2,1,0:T(2,128)S(1)} %broadcast_in_dim.49), channel_id=1, replica_groups=mesh['gx_0'=4,'gx_1'=4,'gy_0'=16,'gy_1'=2] {'gx_0','gx_1','gy_1'}, dimensions={0} | all-to-all | bytes 65536 | tf_op jit(solution)/shard_map/all_to_all | solution.py:18
  151.2 16.8 %all_to_all.52 = f32[16,2,128]{2,1,0:T(2,128)S(1)} all-to-all(f32[16,2,128]{2,1,0:T(2,128)S(1)} %broadcast_in_dim.50), channel_id=1, replica_groups=mesh['gx_0'=4,'gx_1'=4,'gy_0'=16,'gy_1'=2] {'gy_0'}, dimensions={0} | all-to-all | bytes 32768 | tf_op jit(solution)/shard_map/all_to_all | solution.py:18
  168.1 0.7 divide_convert_fusion
  168.8 0.6 pad_maximum_fusion.2
  (22 shorter events, 0.4 us)
Async XLA Ops:
  0.6 2.9 %copy-start = (bf16[2048,128]{1,0:T(8,128)(2,1)S(1)}, bf16[2048,128]{1,0:T(8,128)(2,1)}, u32[]{:S(2)}) copy-start(bf16[2048,128]{1,0:T(8,128)(2,1)} %param.7) | copy-start | bytes 1572868
  3.5 16.5 %copy-start.4 = (f32[16,128]{1,0:T(8,128)S(1)}, f32[16,128]{1,0:T(8,128)}, u32[]{:S(2)}) copy-start(f32[16,128]{1,0:T(8,128)} %get-tuple-element.17) | copy-start | bytes 24580
  3.5 57.4 %copy-start.1 = (bf16[16,3,128,128]{3,2,1,0:T(8,128)(2,1)S(1)}, bf16[16,3,128,128]{3,2,1,0:T(8,128)(2,1)}, u32[]{:S(2)}) copy-start(bf16[16,3,128,128]{3,2,1,0:T(8,128)(2,1)} %tiles.5) | copy-start | bytes 4718596
  3.5 57.4 %copy-start.2 = (s32[16,3]{0,1:T(4,128)S(1)}, s32[16,3]{0,1:T(4,128)}, u32[]{:S(2)}) copy-start(s32[16,3]{0,1:T(4,128)} %param.5) | copy-start | bytes 580
  3.5 57.4 %copy-start.3 = (s32[16,1]{0,1:T(1,128)S(1)}, s32[16,1]{0,1:T(1,128)}, u32[]{:S(2)}) copy-start(s32[16,1]{0,1:T(1,128)} %param.6) | copy-start | bytes 196
  20.7 29.8 %all-to-all-start.1 = ((f32[32,1,256]{2,1,0:T(1,128)}), f32[32,1,256]{2,1,0:T(1,128)S(1)}, u32[]{:S(2)}, u32[]{:S(2)}) async-start(f32[32,1,256]{2,1,0:T(1,128)} %broadcast_in_dim.21), calls=%async_computation.1 | async-start | bytes 65536 | tf_op jit(solution)/shard_map/all_to_all | solution.py:18
  62.2 5.5 %collective-permute-start = (bf16[1024,128]{1,0:T(8,128)(2,1)S(1)}, bf16[1024,128]{1,0:T(8,128)(2,1)S(1)}, u32[]{:S(2)}, u32[]{:S(2)}) collective-permute-start(bf16[1024,128]{1,0:T(8,128)(2,1)S(1)} %get-tuple-element.21), channel_id=1, source_target_pairs={{0,1},{1,0},{2,3},{3,2},{4,5},{5,4},{6,7},{7,6},{8,9},{9,8},{10,11... | collective-permute-start | bytes 786440 | tf_op jit(solution)/shard_map/ppermute | solution.py:144
  105.5 11.2 %collective-permute-start.1 = (bf16[1024,128]{1,0:T(8,128)(2,1)S(1)}, bf16[1024,128]{1,0:T(8,128)(2,1)S(1)}, u32[]{:S(2)}, u32[]{:S(2)}) collective-permute-start(bf16[1024,128]{1,0:T(8,128)(2,1)S(1)} %get-tuple-element.26), channel_id=1, source_target_pairs={{0,1},{1,0},{2,3},{3,2},{4,5},{5,4},{6,7},{7,6},{8,9},{9,8},{10,11... | collective-permute-start | bytes 786440 | tf_op jit(solution)/shard_map/ppermute | solution.py:144

commit v5 on v4

v5 whole, which is shorter than its diff:
```python
import functools

import jax
import jax.numpy as jnp
from jax import lax
from jax.experimental import pallas as pl
from jax.experimental.pallas import tpu as pltpu
from jax.sharding import Mesh
from jax.sharding import PartitionSpec as P

GX = ("gx_0", "gx_1")
GY = ("gy_0", "gy_1")
EVERY = ("gx_0", "gx_1", "gy_0", "gy_1")
Z = "gy_0"
CORE = "gy_1"
PLANE = ("gx_0", "gx_1", "gy_1")


def exchange(array, axis):
    return lax.all_to_all(array, axis, 0, 0, tiled=True)


def from_everyone(array, axis):
    peers = lax.axis_size(axis)
    return exchange(jnp.broadcast_to(array[None], (peers, *array.shape)), axis)


def row_sum_kernel(counts, start, tiles, out, sent, held, arrived):
    here, slots, side, _ = tiles.shape
    groups, rows, _ = sent.shape
    share = start.shape[1]
    half = pl.program_id(0)
    copy = pltpu.make_async_copy(
        start.at[pl.ds(lax.axis_index(CORE) * groups, groups)],
        sent.at[:, pl.ds(0, share), :],
        arrived,
    )

    @pl.when(half == 0)
    def _():
        copy.start()

    mine = lax.broadcasted_iota(jnp.int32, (1, side), 1) // share == half
    row = lax.broadcasted_iota(jnp.int32, (rows - share, side), 0)
    ones = jnp.ones((side, side), tiles.dtype)
    down = lax.broadcasted_iota(jnp.int32, (side, side), 0)
    across = lax.broadcasted_iota(jnp.int32, (side, side), 1)
    for t in range(here):
        which = lax.broadcasted_iota(jnp.int32, counts.shape, 1) == half * here + t
        count = jnp.sum(jnp.where(which, counts[...], 0), axis=1, keepdims=True)
        total = jnp.zeros((side, side), jnp.float32)
        for s in range(slots):
            part = jnp.dot(tiles[t, s], ones, preferred_element_type=jnp.float32)
            total = total + jnp.where(s < count, part, 0.0)
        sums = jnp.sum(jnp.where(down == across, total, 0.0), axis=0, keepdims=True)
        out[pl.ds(half * here + t, 1)] = sums
        turned = pltpu.roll(sums, share, 1)
        for part in range(2):
            at = pl.ds(2 * t + part, 1)
            held[at] = jnp.where(
                mine, jnp.where(half == part, sums, turned), held[at]
            )

    @pl.when(half == 1)
    def _():
        for p in range(2 * here):
            value = held[p : p + 1]
            high = value.astype(sent.dtype).astype(jnp.float32)
            middle = (value - high).astype(sent.dtype).astype(jnp.float32)
            low = value - high - middle
            block = jnp.where(row == 1, middle, jnp.where(row == 2, low, 0.0))
            sent[p, share:] = jnp.where(row == 0, high, block).astype(sent.dtype)
        copy.wait()


def spread_kernel(terms, own, out):
    for p in range(terms.shape[0]):
        part = jnp.sum(terms[p].astype(jnp.float32), axis=0, keepdims=True)
        line = jnp.concatenate([part, own[p : p + 1]], axis=1)
        out[2 * p] = line
        out[2 * p + 1] = line


def pick(cols, counts, column, r, slots, side):
    parts = []
    for s in range(slots):
        start = pl.multiple_of(cols[s, r] * side, side)
        part = column[pl.ds(start, side), :]
        live = s < counts[0, r]
        parts.append(jnp.where(live, part, jnp.zeros_like(part)))
    return jnp.concatenate(parts, axis=0)


def first_kernel(flip, place, cols, counts, tiles, column, out):
    row_tiles, slots, side, _ = tiles.shape
    half = row_tiles // 2
    core = 1 - place[0] if flip else place[0]
    for t in range(half):
        r = core * half + t
        wide = jnp.concatenate([tiles[r, s] for s in range(slots)], axis=1)
        out[t * side : (t + 1) * side, :] = jnp.dot(
            wide,
            pick(cols, counts, column, r, slots, side),
            preferred_element_type=jnp.float32,
        ).astype(out.dtype)


def second_kernel(flip, place, cols, counts, tiles, column, out):
    row_tiles, slots, side, _ = tiles.shape
    half = row_tiles // 2
    share = side // 2
    part = 1 - place[0] if flip else place[0]
    rows = pl.ds(pl.multiple_of(part * share, share), share)
    for r in range(row_tiles):
        picked = pick(cols, counts, column, r, slots, side)
        diagonal = (place[1] == place[2]) & (place[0] == r // half)
        wide = jnp.concatenate([tiles[r, s, rows, :] for s in range(slots)], axis=1)
        own = column[pl.ds((r % half) * side + part * share, share), :]
        value = jnp.dot(wide, picked, preferred_element_type=jnp.float32)
        value = value + jnp.where(diagonal, own.astype(jnp.float32), 0.0)
        out[r * share : (r + 1) * share, :] = value.astype(out.dtype)


SMEM = pl.BlockSpec(memory_space=pltpu.SMEM)
VMEM = pl.BlockSpec(memory_space=pltpu.VMEM)
PARAMS = pltpu.CompilerParams(vmem_limit_bytes=24 << 20)
COST = pl.CostEstimate(flops=800 << 20, bytes_accessed=2 << 20, transcendentals=0)


def on_device(tiles, tile_cols, row_counts, start_block):
    row_tiles, slot_count, side, _ = tiles.shape
    width = start_block.shape[1]
    groups = lax.axis_size(GX)
    half_tiles = row_tiles // 2
    local_rows = row_tiles * side
    half_rows = local_rows // 2
    share = half_rows // groups
    nodes = local_rows * groups
    core = lax.axis_index(CORE)
    line = lax.axis_index(GX)
    plane = lax.axis_index(Z)
    f32, bf16 = jnp.float32, jnp.bfloat16

    place = jnp.stack([core, line, plane]).astype(jnp.int32)
    cols = tile_cols.T
    counts = row_counts.T
    steps = 2
    row_sums, sent = pl.pallas_call(
        row_sum_kernel,
        grid=(steps,),
        out_shape=[
            jax.ShapeDtypeStruct((row_tiles, side), f32),
            jax.ShapeDtypeStruct((groups, share + 16, side), bf16),
        ],
        in_specs=[
            pl.BlockSpec((1, row_tiles), lambda g: (0, 0)),
            pl.BlockSpec(memory_space=pl.ANY),
            pl.BlockSpec(
                (row_tiles // steps, slot_count, side, side), lambda g: (g, 0, 0, 0)
            ),
        ],
        out_specs=[pl.BlockSpec((row_tiles, side), lambda g: (0, 0)), VMEM],
        scratch_shapes=[
            pltpu.VMEM((groups, side), f32),
            pltpu.SemaphoreType.DMA(()),
        ],
    )(counts, start_block.reshape(2 * groups, share, width), tiles)

    def swapped(array):
        return lax.ppermute(array, CORE, [(0, 1), (1, 0)])

    at_seg = core * share
    at_own = side + at_seg
    sent, place, at_seg, at_own = lax.optimization_barrier((sent, place, at_seg, at_own))
    got = exchange(sent, GX)
    start_seg = lax.dynamic_index_in_dim(got, plane, 0, keepdims=False)[:share]

    both = pl.pallas_call(
        spread_kernel,
        grid=(1,),
        out_shape=jax.ShapeDtypeStruct((2 * groups, 1, 2 * side), f32),
        in_specs=[
            pl.BlockSpec((groups, 16, side), lambda g: (0, share // 16, 0)),
            VMEM,
        ],
        out_specs=VMEM,
        compiler_params=PARAMS,
    )(got, row_sums)
    degree = 1.0 + exchange(both, GY).sum(axis=(0, 1))
    scale = 1.0 / jnp.sqrt(degree)
    scale_seg = lax.dynamic_slice_in_dim(scale, at_seg, share, 0)
    scale_own = lax.dynamic_slice_in_dim(scale, at_own, share, 0)

    def pair_sum(kernel, column):
        def products(flip, kind):
            return pl.pallas_call(
                functools.partial(kernel, flip),
                out_shape=jax.ShapeDtypeStruct((half_rows, width), kind),
                in_specs=[SMEM] * 3 + [VMEM] * 2,
                out_specs=VMEM,
                compiler_params=PARAMS,
                cost_estimate=COST,
            )(place, cols, counts, tiles, column)

        arrived = swapped(products(True, bf16))
        return products(False, f32) + arrived.astype(f32)

    u_seg = (scale_seg[:, None] * start_seg.astype(f32)).astype(bf16)
    u = from_everyone(u_seg, GX).reshape(half_rows, width)
    pair = pair_sum(first_kernel, u)
    chunks = pair.astype(bf16).reshape(groups, share, width)
    product = exchange(exchange(chunks, GX), Z).astype(f32).sum(axis=0)
    w1 = scale_seg[:, None] * (product + u_seg.astype(f32))
    squares1 = jnp.sum(w1 * w1, axis=0)

    v_seg = (scale_seg[:, None] * w1).astype(bf16)
    v_seg, squares1, scale_own = lax.optimization_barrier((v_seg, squares1, scale_own))
    v = from_everyone(v_seg, GX).reshape(half_rows, width)
    pair = pair_sum(second_kernel, v).reshape(row_tiles, share, width)
    product = exchange(pair.astype(bf16), Z).astype(f32).sum(axis=0)
    w2 = scale_own[:, None] * product
    squares2 = jnp.sum(w2 * w2, axis=0)

    squares = jnp.stack([squares1, squares2])
    squares = from_everyone(squares, PLANE).sum(axis=0)
    squares = from_everyone(squares, Z).sum(axis=0)
    spread1 = jnp.sqrt(squares[0] / nodes + 1e-06)
    spread2 = jnp.sqrt(squares[1] / (spread1 * spread1) / nodes + 1e-06)
    vectors = (w2 / (spread1 * spread2)).astype(bf16)
    return (vectors, jnp.stack([spread1, spread2]))


def solution(mesh):
    torus = Mesh(mesh.devices.reshape(4, 4, 16, 2), EVERY)
    placed = (P(GX, GY, None, None), P(GX, GY), P(GX, GY), P(GX, None))
    return jax.shard_map(
        on_device,
        mesh=torus,
        in_specs=placed,
        out_specs=(P(EVERY, None), P()),
        check_vma=False,
    )
```

time: 170 us -> 170 us (level)
  Pallas kernels: 5.36 us -> 7.85 us
  waiting for transfers between devices: 14.4 us -> 12.4 us
    pallas_call x2 -> x5, Pallas kernels: 2.5 us -> 4.68 us  [the longest x4 4.04 us: products(): pl.pallas_call(functools.partial(kernel, flip), out_shape=jax.ShapeDtypeS...]
    ppermute x2, waiting for transfers between devices: 2.28 us -> 0.24 us  [swapped(): return lax.ppermute(array, CORE, [(0, 1), (1, 0)])]
  transfers between devices with their start and end apart: 3 -> 3, of which waited for: 3 -> 3; matrix products, arithmetic and copies ran while one was open for 0% -> 0% of each run, Pallas kernels for 0% -> 1%
where the time goes in v5:
time: 170 us; the launch traced here: 169 us
  blocking collectives  113 us (66%)
  starting transfers between devices  32.1 us (19%)
  waiting for transfers between devices  12.4 us (7%)
  Pallas kernels  7.85 us (5%)
  other arithmetic  1.97 us (1%)
    all_to_all x8, blocking collectives, exchange(): return lax.all_to_all(array, axis, 0, 0, tiled=True)  113 us
    all_to_all x1, starting transfers between devices, exchange(): return lax.all_to_all(array, axis, 0, 0, tiled=True)  17.7 us
    ppermute x2, starting transfers between devices, swapped(): return lax.ppermute(array, CORE, [(0, 1), (1, 0)])  14.4 us
    all_to_all x1, waiting for transfers between devices, exchange(): return lax.all_to_all(array, axis, 0, 0, tiled=True)  12.1 us
    pallas_call x4, Pallas kernels, products(): pl.pallas_call(functools.partial(kernel, flip), out_shape=jax.ShapeDtypeS...  4.04 us
  transfers between devices with their start and end apart: 3, of which 3 were waited for; matrix products, arithmetic and copies ran while one was open for 0% of the time, Pallas kernels for 1%

profile of v5, /device:TPU:1, one launch (start us, length us, event | category | flops | bytes accessed | tf_op | source)
XLA Modules:
  0.0 169.0 jit_solution(15551849797282483100)
XLA Ops:
  0.6 0.1 pad_add_fusion.place
  0.7 3.2 %shard_map.59 = (f32[16,128]{1,0:T(8,128)}, bf16[16,80,128]{2,1,0:T(8,128)(2,1)}) custom-call(s32[1,16]{1,0:T(1,128)} %bitcast.30, bf16[32,64,128]{2,1,0:T(8,128)(2,1)} %bitcast.41, bf16[16,3,128,128]{3,2,1,0:T(8,128)(2,1)} %tiles.9), custom_call_target="tpu_custom_call" | custom-call | tf_op jit(solution)/shard_map/pallas_call | solution.py:148
  3.9 15.5 %all_to_all.45.terms = bf16[16,80,128]{2,1,0:T(8,128)(2,1)S(1)} all-to-all(bf16[16,80,128]{2,1,0:T(8,128)(2,1)} %get-tuple-element.12), channel_id=1, replica_groups=mesh['gx_0'=4,'gx_1'=4,'gy_0'=16,'gy_1'=2] {'gx_0','gx_1'}, dimensions={0} | all-to-all | bytes 655360 | tf_op jit(solution)/shard_map/all_to_all | solution.py:20
  19.4 0.7 copy-done.1
  20.1 0.6 shard_map.60
  20.7 17.7 %all-to-all-start.1 = ((f32[32,1,256]{2,1,0:T(1,128)}), f32[32,1,256]{2,1,0:T(1,128)S(1)}, u32[]{:S(2)}, u32[]{:S(2)}) async-start(f32[32,1,256]{2,1,0:T(1,128)} %shard_map.60), calls=%async_computation.1 | async-start | bytes 65536 | tf_op jit(solution)/shard_map/all_to_all | solution.py:20
  38.4 12.1 %all-to-all-done.1 = f32[32,1,256]{2,1,0:T(1,128)S(1)} async-done(((f32[32,1,256]{2,1,0:T(1,128)}), f32[32,1,256]{2,1,0:T(1,128)S(1)}, u32[]{:S(2)}, u32[]{:S(2)}) %all-to-all-start.1) | async-done | bytes 32800 | tf_op jit(solution)/shard_map/all_to_all | solution.py:20
  50.5 0.1 reduce_sum.63
  50.6 0.1 fusion.4
  50.7 0.1 fusion.3
  50.8 10.2 %all_to_all.46 = bf16[16,64,128]{2,1,0:T(8,128)(2,1)S(1)} all-to-all(bf16[16,64,128]{2,1,0:T(8,128)(2,1)S(1)} %broadcast_in_dim.11), channel_id=1, replica_groups=mesh['gx_0'=4,'gx_1'=4,'gy_0'=16,'gy_1'=2] {'gx_0','gx_1'}, dimensions={0} | all-to-all | bytes 524288 | tf_op jit(solution)/shard_map/all_to_all | solution.py:20
  61.0 0.0 copy-done.2
  61.0 1.0 shard_map.62
  62.0 4.4 %collective-permute-start = (bf16[1024,128]{1,0:T(8,128)(2,1)S(1)}, bf16[1024,128]{1,0:T(8,128)(2,1)S(1)}, u32[]{:S(2)}, u32[]{:S(2)}) collective-permute-start(bf16[1024,128]{1,0:T(8,128)(2,1)S(1)} %shard_map.62), channel_id=1, source_target_pairs={{0,1},{1,0},{2,3},{3,2},{4,5},{5,4},{6,7},{7,6},{8,9},{9,8},{10,11... | collective-permute-start | bytes 786440 | tf_op jit(solution)/shard_map/ppermute | solution.py:170
  66.4 1.0 shard_map.61
  67.4 0.2 collective-permute-done
  67.5 0.1 add_convert_fusion.1
  67.6 10.7 %all_to_all.47 = bf16[16,64,128]{2,1,0:T(8,128)(2,1)S(1)} all-to-all(bf16[16,64,128]{2,1,0:T(8,128)(2,1)S(1)} %bitcast.39), channel_id=1, replica_groups=mesh['gx_0'=4,'gx_1'=4,'gy_0'=16,'gy_1'=2] {'gx_0','gx_1'}, dimensions={0} | all-to-all | bytes 524288 | tf_op jit(solution)/shard_map/all_to_all | solution.py:20
  78.3 15.4 %all_to_all.48 = bf16[16,64,128]{2,1,0:T(8,128)(2,1)S(1)} all-to-all(bf16[16,64,128]{2,1,0:T(8,128)(2,1)S(1)} %all_to_all.47), channel_id=1, replica_groups=mesh['gx_0'=4,'gx_1'=4,'gy_0'=16,'gy_1'=2] {'gy_0'}, dimensions={0} | all-to-all | bytes 524288 | tf_op jit(solution)/shard_map/all_to_all | solution.py:20
  93.8 0.1 multiply_reduce_fusion.1
  93.9 10.1 %all_to_all.49 = bf16[16,64,128]{2,1,0:T(8,128)(2,1)S(1)} all-to-all(bf16[16,64,128]{2,1,0:T(8,128)(2,1)S(1)} %broadcast_in_dim.12), channel_id=1, replica_groups=mesh['gx_0'=4,'gx_1'=4,'gy_0'=16,'gy_1'=2] {'gx_0','gx_1'}, dimensions={0} | all-to-all | bytes 524288 | tf_op jit(solution)/shard_map/all_to_all | solution.py:20
  104.1 1.1 shard_map.64
  105.1 10.0 %collective-permute-start.1 = (bf16[1024,128]{1,0:T(8,128)(2,1)S(1)}, bf16[1024,128]{1,0:T(8,128)(2,1)S(1)}, u32[]{:S(2)}, u32[]{:S(2)}) collective-permute-start(bf16[1024,128]{1,0:T(8,128)(2,1)S(1)} %shard_map.64), channel_id=1, source_target_pairs={{0,1},{1,0},{2,3},{3,2},{4,5},{5,4},{6,7},{7,6},{8,9},{9,8},{10,11... | collective-permute-start | bytes 786440 | tf_op jit(solution)/shard_map/ppermute | solution.py:170
  115.2 1.1 shard_map.63
  116.2 0.1 collective-permute-done.1
  116.3 0.1 add_convert_fusion
  116.4 18.9 %all_to_all.50 = bf16[16,64,128]{2,1,0:T(8,128)(2,1)S(1)} all-to-all(bf16[16,64,128]{2,1,0:T(8,128)(2,1)S(1)} %bitcast.40), channel_id=1, replica_groups=mesh['gx_0'=4,'gx_1'=4,'gy_0'=16,'gy_1'=2] {'gy_0'}, dimensions={0} | all-to-all | bytes 524288 | tf_op jit(solution)/shard_map/all_to_all | solution.py:20
  135.3 0.1 multiply_reduce_fusion
  135.4 15.4 %all_to_all.51 = f32[32,2,128]{2,1,0:T(2,128)S(1)} all-to-all(f32[32,2,128]{2,1,0:T(2,128)S(1)} %broadcast_in_dim.13), channel_id=1, replica_groups=mesh['gx_0'=4,'gx_1'=4,'gy_0'=16,'gy_1'=2] {'gx_0','gx_1','gy_1'}, dimensions={0} | all-to-all | bytes 65536 | tf_op jit(solution)/shard_map/all_to_all | solution.py:20
  150.8 16.8 %all_to_all.52 = f32[16,2,128]{2,1,0:T(2,128)S(1)} all-to-all(f32[16,2,128]{2,1,0:T(2,128)S(1)} %broadcast_in_dim.14), channel_id=1, replica_groups=mesh['gx_0'=4,'gx_1'=4,'gy_0'=16,'gy_1'=2] {'gy_0'}, dimensions={0} | all-to-all | bytes 32768 | tf_op jit(solution)/shard_map/all_to_all | solution.py:20
  167.7 0.7 divide_convert_fusion
  168.4 0.6 pad_maximum_fusion.1
  (17 shorter events, 0.3 us)
Async XLA Ops:
  0.7 60.3 %copy-start = (bf16[16,3,128,128]{3,2,1,0:T(8,128)(2,1)S(1)}, bf16[16,3,128,128]{3,2,1,0:T(8,128)(2,1)}, u32[]{:S(2)}) copy-start(bf16[16,3,128,128]{3,2,1,0:T(8,128)(2,1)} %tiles.9) | copy-start | bytes 4718596
  0.7 60.3 %copy-start.2 = (s32[16,1]{0,1:T(1,128)S(1)}, s32[16,1]{0,1:T(1,128)}, u32[]{:S(2)}) copy-start(s32[16,1]{0,1:T(1,128)} %param.6) | copy-start | bytes 196
  0.7 60.3 %copy-start.3 = (s32[16,3]{0,1:T(4,128)S(1)}, s32[16,3]{0,1:T(4,128)}, u32[]{:S(2)}) copy-start(s32[16,3]{0,1:T(4,128)} %param.5) | copy-start | bytes 580
  19.4 0.7 copy-start.1
  20.7 29.8 %all-to-all-start.1 = ((f32[32,1,256]{2,1,0:T(1,128)}), f32[32,1,256]{2,1,0:T(1,128)S(1)}, u32[]{:S(2)}, u32[]{:S(2)}) async-start(f32[32,1,256]{2,1,0:T(1,128)} %shard_map.60), calls=%async_computation.1 | async-start | bytes 65536 | tf_op jit(solution)/shard_map/all_to_all | solution.py:20
  62.0 5.5 %collective-permute-start = (bf16[1024,128]{1,0:T(8,128)(2,1)S(1)}, bf16[1024,128]{1,0:T(8,128)(2,1)S(1)}, u32[]{:S(2)}, u32[]{:S(2)}) collective-permute-start(bf16[1024,128]{1,0:T(8,128)(2,1)S(1)} %shard_map.62), channel_id=1, source_target_pairs={{0,1},{1,0},{2,3},{3,2},{4,5},{5,4},{6,7},{7,6},{8,9},{9,8},{10,11... | collective-permute-start | bytes 786440 | tf_op jit(solution)/shard_map/ppermute | solution.py:170
  105.1 11.2 %collective-permute-start.1 = (bf16[1024,128]{1,0:T(8,128)(2,1)S(1)}, bf16[1024,128]{1,0:T(8,128)(2,1)S(1)}, u32[]{:S(2)}, u32[]{:S(2)}) collective-permute-start(bf16[1024,128]{1,0:T(8,128)(2,1)S(1)} %shard_map.64), channel_id=1, source_target_pairs={{0,1},{1,0},{2,3},{3,2},{4,5},{5,4},{6,7},{7,6},{8,9},{9,8},{10,11... | collective-permute-start | bytes 786440 | tf_op jit(solution)/shard_map/ppermute | solution.py:170

commit v6 on v5

--- a/solution.py
+++ b/solution.py
@@ -121,6 +121,15 @@
         out[r * share : (r + 1) * share, :] = value.astype(out.dtype)
 
 
+def last_kernel(nodes, squares, w2, vectors, spreads):
+    total = jnp.sum(squares[...], axis=0)
+    first = jnp.sqrt(total[0:1] / nodes + 1e-06)
+    second = jnp.sqrt(total[1:2] / (first * first) / nodes + 1e-06)
+    vectors[...] = (w2[...] / (first * second)).astype(vectors.dtype)
+    spreads[0:1] = first
+    spreads[1:2] = second
+
+
 SMEM = pl.BlockSpec(memory_space=pltpu.SMEM)
 VMEM = pl.BlockSpec(memory_space=pltpu.VMEM)
 PARAMS = pltpu.CompilerParams(vmem_limit_bytes=24 << 20)
@@ -223,11 +232,18 @@
 
     squares = jnp.stack([squares1, squares2])
     squares = from_everyone(squares, PLANE).sum(axis=0)
-    squares = from_everyone(squares, Z).sum(axis=0)
-    spread1 = jnp.sqrt(squares[0] / nodes + 1e-06)
-    spread2 = jnp.sqrt(squares[1] / (spread1 * spread1) / nodes + 1e-06)
-    vectors = (w2 / (spread1 * spread2)).astype(bf16)
-    return (vectors, jnp.stack([spread1, spread2]))
+    return tuple(
+        pl.pallas_call(
+            functools.partial(last_kernel, nodes),
+            out_shape=[
+                jax.ShapeDtypeStruct((share, width), bf16),
+                jax.ShapeDtypeStruct((2, width), f32),
+            ],
+            in_specs=[VMEM] * 2,
+            out_specs=[VMEM] * 2,
+            compiler_params=PARAMS,
+        )(from_everyone(squares, Z), w2)
+    )
 
 
 def solution(mesh):

time: 170 us -> 169 us (level)
  no operation moved by 1% of the time
where the time goes in v6:
time: 169 us; the launch traced here: 168 us
  blocking collectives  113 us (67%)
  starting transfers between devices  32.1 us (19%)
  waiting for transfers between devices  12.4 us (7%)
  Pallas kernels  8.51 us (5%)
    all_to_all x8, blocking collectives, exchange(): return lax.all_to_all(array, axis, 0, 0, tiled=True)  113 us
    all_to_all x1, starting transfers between devices, exchange(): return lax.all_to_all(array, axis, 0, 0, tiled=True)  17.7 us
    ppermute x2, starting transfers between devices, swapped(): return lax.ppermute(array, CORE, [(0, 1), (1, 0)])  14.4 us
    all_to_all x1, waiting for transfers between devices, exchange(): return lax.all_to_all(array, axis, 0, 0, tiled=True)  12.1 us
    pallas_call x4, Pallas kernels, products(): pl.pallas_call(functools.partial(kernel, flip), out_shape=jax.ShapeDtypeS...  4.03 us
  transfers between devices with their start and end apart: 3, of which 3 were waited for; matrix products, arithmetic and copies ran while one was open for 0% of the time, Pallas kernels for 1%

profile of v6, /device:TPU:1, one launch (start us, length us, event | category | flops | bytes accessed | tf_op | source)
XLA Modules:
  0.0 168.3 jit_solution(9891631008372651639)
XLA Ops:
  0.6 0.1 pad_add_fusion.place
  0.7 3.2 %shard_map.59 = (f32[16,128]{1,0:T(8,128)}, bf16[16,80,128]{2,1,0:T(8,128)(2,1)}) custom-call(s32[1,16]{1,0:T(1,128)} %bitcast.28, bf16[32,64,128]{2,1,0:T(8,128)(2,1)} %bitcast.39, bf16[16,3,128,128]{3,2,1,0:T(8,128)(2,1)} %tiles.9), custom_call_target="tpu_custom_call" | custom-call | tf_op jit(solution)/shard_map/pallas_call | solution.py:157
  3.9 15.5 %all_to_all.45.terms = bf16[16,80,128]{2,1,0:T(8,128)(2,1)S(1)} all-to-all(bf16[16,80,128]{2,1,0:T(8,128)(2,1)} %get-tuple-element.12), channel_id=1, replica_groups=mesh['gx_0'=4,'gx_1'=4,'gy_0'=16,'gy_1'=2] {'gx_0','gx_1'}, dimensions={0} | all-to-all | bytes 655360 | tf_op jit(solution)/shard_map/all_to_all | solution.py:20
  19.4 0.7 copy-done.1
  20.1 0.6 shard_map.60
  20.7 17.7 %all-to-all-start.1 = ((f32[32,1,256]{2,1,0:T(1,128)}), f32[32,1,256]{2,1,0:T(1,128)S(1)}, u32[]{:S(2)}, u32[]{:S(2)}) async-start(f32[32,1,256]{2,1,0:T(1,128)} %shard_map.60), calls=%async_computation.1 | async-start | bytes 65536 | tf_op jit(solution)/shard_map/all_to_all | solution.py:20
  38.4 12.1 %all-to-all-done.1 = f32[32,1,256]{2,1,0:T(1,128)S(1)} async-done(((f32[32,1,256]{2,1,0:T(1,128)}), f32[32,1,256]{2,1,0:T(1,128)S(1)}, u32[]{:S(2)}, u32[]{:S(2)}) %all-to-all-start.1) | async-done | bytes 32800 | tf_op jit(solution)/shard_map/all_to_all | solution.py:20
  50.5 0.1 reduce_sum.54
  50.6 0.1 fusion.4
  50.7 0.1 fusion.3
  50.8 10.2 %all_to_all.46 = bf16[16,64,128]{2,1,0:T(8,128)(2,1)S(1)} all-to-all(bf16[16,64,128]{2,1,0:T(8,128)(2,1)S(1)} %broadcast_in_dim.11), channel_id=1, replica_groups=mesh['gx_0'=4,'gx_1'=4,'gy_0'=16,'gy_1'=2] {'gx_0','gx_1'}, dimensions={0} | all-to-all | bytes 524288 | tf_op jit(solution)/shard_map/all_to_all | solution.py:20
  61.0 0.0 copy-done
  61.0 0.0 copy-done.2
  61.0 1.0 shard_map.62
  62.0 4.4 %collective-permute-start = (bf16[1024,128]{1,0:T(8,128)(2,1)S(1)}, bf16[1024,128]{1,0:T(8,128)(2,1)S(1)}, u32[]{:S(2)}, u32[]{:S(2)}) collective-permute-start(bf16[1024,128]{1,0:T(8,128)(2,1)S(1)} %shard_map.62), channel_id=1, source_target_pairs={{0,1},{1,0},{2,3},{3,2},{4,5},{5,4},{6,7},{7,6},{8,9},{9,8},{10,11... | collective-permute-start | bytes 786440 | tf_op jit(solution)/shard_map/ppermute | solution.py:179
  66.4 1.0 shard_map.61
  67.4 0.2 collective-permute-done
  67.5 0.1 add_convert_fusion.1
  67.6 10.7 %all_to_all.47 = bf16[16,64,128]{2,1,0:T(8,128)(2,1)S(1)} all-to-all(bf16[16,64,128]{2,1,0:T(8,128)(2,1)S(1)} %bitcast.37), channel_id=1, replica_groups=mesh['gx_0'=4,'gx_1'=4,'gy_0'=16,'gy_1'=2] {'gx_0','gx_1'}, dimensions={0} | all-to-all | bytes 524288 | tf_op jit(solution)/shard_map/all_to_all | solution.py:20
  78.3 15.4 %all_to_all.48 = bf16[16,64,128]{2,1,0:T(8,128)(2,1)S(1)} all-to-all(bf16[16,64,128]{2,1,0:T(8,128)(2,1)S(1)} %all_to_all.47), channel_id=1, replica_groups=mesh['gx_0'=4,'gx_1'=4,'gy_0'=16,'gy_1'=2] {'gy_0'}, dimensions={0} | all-to-all | bytes 524288 | tf_op jit(solution)/shard_map/all_to_all | solution.py:20
  93.8 0.1 multiply_reduce_fusion.1
  93.9 10.1 %all_to_all.49 = bf16[16,64,128]{2,1,0:T(8,128)(2,1)S(1)} all-to-all(bf16[16,64,128]{2,1,0:T(8,128)(2,1)S(1)} %broadcast_in_dim.12), channel_id=1, replica_groups=mesh['gx_0'=4,'gx_1'=4,'gy_0'=16,'gy_1'=2] {'gx_0','gx_1'}, dimensions={0} | all-to-all | bytes 524288 | tf_op jit(solution)/shard_map/all_to_all | solution.py:20
  104.1 1.1 shard_map.64
  105.1 10.0 %collective-permute-start.1 = (bf16[1024,128]{1,0:T(8,128)(2,1)S(1)}, bf16[1024,128]{1,0:T(8,128)(2,1)S(1)}, u32[]{:S(2)}, u32[]{:S(2)}) collective-permute-start(bf16[1024,128]{1,0:T(8,128)(2,1)S(1)} %shard_map.64), channel_id=1, source_target_pairs={{0,1},{1,0},{2,3},{3,2},{4,5},{5,4},{6,7},{7,6},{8,9},{9,8},{10,11... | collective-permute-start | bytes 786440 | tf_op jit(solution)/shard_map/ppermute | solution.py:179
  115.2 1.1 shard_map.63
  116.2 0.1 collective-permute-done.1
  116.3 0.1 add_convert_fusion
  116.4 18.9 %all_to_all.50 = bf16[16,64,128]{2,1,0:T(8,128)(2,1)S(1)} all-to-all(bf16[16,64,128]{2,1,0:T(8,128)(2,1)S(1)} %bitcast.38), channel_id=1, replica_groups=mesh['gx_0'=4,'gx_1'=4,'gy_0'=16,'gy_1'=2] {'gy_0'}, dimensions={0} | all-to-all | bytes 524288 | tf_op jit(solution)/shard_map/all_to_all | solution.py:20
  135.3 0.1 multiply_reduce_fusion
  135.4 15.4 %all_to_all.51 = f32[32,2,128]{2,1,0:T(2,128)S(1)} all-to-all(f32[32,2,128]{2,1,0:T(2,128)S(1)} %broadcast_in_dim.13), channel_id=1, replica_groups=mesh['gx_0'=4,'gx_1'=4,'gy_0'=16,'gy_1'=2] {'gx_0','gx_1','gy_1'}, dimensions={0} | all-to-all | bytes 65536 | tf_op jit(solution)/shard_map/all_to_all | solution.py:20
  150.8 16.8 %all_to_all.52.squares = f32[16,2,128]{2,1,0:T(2,128)S(1)} all-to-all(f32[16,2,128]{2,1,0:T(2,128)S(1)} %broadcast_in_dim.14), channel_id=1, replica_groups=mesh['gx_0'=4,'gx_1'=4,'gy_0'=16,'gy_1'=2] {'gy_0'}, dimensions={0} | all-to-all | bytes 32768 | tf_op jit(solution)/shard_map/all_to_all | solution.py:20
  167.6 0.7 shard_map.65
  (14 shorter events, 0.3 us)
Async XLA Ops:
  0.7 60.3 %copy-start = (bf16[16,3,128,128]{3,2,1,0:T(8,128)(2,1)S(1)}, bf16[16,3,128,128]{3,2,1,0:T(8,128)(2,1)}, u32[]{:S(2)}) copy-start(bf16[16,3,128,128]{3,2,1,0:T(8,128)(2,1)} %tiles.9) | copy-start | bytes 4718596
  0.7 60.3 %copy-start.2 = (s32[16,1]{0,1:T(1,128)S(1)}, s32[16,1]{0,1:T(1,128)}, u32[]{:S(2)}) copy-start(s32[16,1]{0,1:T(1,128)} %param.6) | copy-start | bytes 196
  0.7 60.3 %copy-start.3 = (s32[16,3]{0,1:T(4,128)S(1)}, s32[16,3]{0,1:T(4,128)}, u32[]{:S(2)}) copy-start(s32[16,3]{0,1:T(4,128)} %param.5) | copy-start | bytes 580
  19.4 0.7 copy-start.1
  20.7 29.8 %all-to-all-start.1 = ((f32[32,1,256]{2,1,0:T(1,128)}), f32[32,1,256]{2,1,0:T(1,128)S(1)}, u32[]{:S(2)}, u32[]{:S(2)}) async-start(f32[32,1,256]{2,1,0:T(1,128)} %shard_map.60), calls=%async_computation.1 | async-start | bytes 65536 | tf_op jit(solution)/shard_map/all_to_all | solution.py:20
  62.0 5.5 %collective-permute-start = (bf16[1024,128]{1,0:T(8,128)(2,1)S(1)}, bf16[1024,128]{1,0:T(8,128)(2,1)S(1)}, u32[]{:S(2)}, u32[]{:S(2)}) collective-permute-start(bf16[1024,128]{1,0:T(8,128)(2,1)S(1)} %shard_map.62), channel_id=1, source_target_pairs={{0,1},{1,0},{2,3},{3,2},{4,5},{5,4},{6,7},{7,6},{8,9},{9,8},{10,11... | collective-permute-start | bytes 786440 | tf_op jit(solution)/shard_map/ppermute | solution.py:179
  105.1 11.2 %collective-permute-start.1 = (bf16[1024,128]{1,0:T(8,128)(2,1)S(1)}, bf16[1024,128]{1,0:T(8,128)(2,1)S(1)}, u32[]{:S(2)}, u32[]{:S(2)}) collective-permute-start(bf16[1024,128]{1,0:T(8,128)(2,1)S(1)} %shard_map.64), channel_id=1, source_target_pairs={{0,1},{1,0},{2,3},{3,2},{4,5},{5,4},{6,7},{7,6},{8,9},{9,8},{10,11... | collective-permute-start | bytes 786440 | tf_op jit(solution)/shard_map/ppermute | solution.py:179

commit v7 on v6

--- a/solution.py
+++ b/solution.py
@@ -168,7 +168,8 @@
                 (row_tiles // steps, slot_count, side, side), lambda g: (g, 0, 0, 0)
             ),
         ],
-        out_specs=[pl.BlockSpec((row_tiles, side), lambda g: (0, 0)), VMEM],
+        out_specs=[VMEM] * 2,
+        compiler_params=pltpu.CompilerParams(vmem_limit_bytes=63 << 20),
         scratch_shapes=[
             pltpu.VMEM((groups, side), f32),
             pltpu.SemaphoreType.DMA(()),

time: 169 us -> 169 us (level)
  no operation moved by 1% of the time
where the time goes in v7:
time: 169 us; the launch traced here: 168 us
  blocking collectives  113 us (67%)
  starting transfers between devices  32.1 us (19%)
  waiting for transfers between devices  12.4 us (7%)
  Pallas kernels  8.42 us (5%)
    all_to_all x8, blocking collectives, exchange(): return lax.all_to_all(array, axis, 0, 0, tiled=True)  113 us
    all_to_all x1, starting transfers between devices, exchange(): return lax.all_to_all(array, axis, 0, 0, tiled=True)  17.7 us
    ppermute x2, starting transfers between devices, swapped(): return lax.ppermute(array, CORE, [(0, 1), (1, 0)])  14.4 us
    all_to_all x1, waiting for transfers between devices, exchange(): return lax.all_to_all(array, axis, 0, 0, tiled=True)  12.1 us
    pallas_call x4, Pallas kernels, products(): pl.pallas_call(functools.partial(kernel, flip), out_shape=jax.ShapeDtypeS...  4.04 us
  transfers between devices with their start and end apart: 3, of which 3 were waited for; matrix products, arithmetic and copies ran while one was open for 0% of the time, Pallas kernels for 1%

profile of v7, /device:TPU:1, one launch (start us, length us, event | category | flops | bytes accessed | tf_op | source)
XLA Modules:
  0.0 168.4 jit_solution(8846643200774186835)
XLA Ops:
  0.6 0.1 pad_add_fusion.place
  0.7 3.1 %shard_map.59 = (f32[16,128]{1,0:T(8,128)}, bf16[16,80,128]{2,1,0:T(8,128)(2,1)}) custom-call(s32[1,16]{1,0:T(1,128)} %bitcast.28, bf16[32,64,128]{2,1,0:T(8,128)(2,1)} %bitcast.39, bf16[16,3,128,128]{3,2,1,0:T(8,128)(2,1)} %tiles.9), custom_call_target="tpu_custom_call" | custom-call | tf_op jit(solution)/shard_map/pallas_call | solution.py:157
  3.8 0.0 copy-start
  3.8 15.6 %all_to_all.45.terms = bf16[16,80,128]{2,1,0:T(8,128)(2,1)S(1)} all-to-all(bf16[16,80,128]{2,1,0:T(8,128)(2,1)} %get-tuple-element.12), channel_id=1, replica_groups=mesh['gx_0'=4,'gx_1'=4,'gy_0'=16,'gy_1'=2] {'gx_0','gx_1'}, dimensions={0} | all-to-all | bytes 655360 | tf_op jit(solution)/shard_map/all_to_all | solution.py:20
  19.4 0.7 copy-done.1
  20.1 0.6 shard_map.60
  20.8 17.7 %all-to-all-start.1 = ((f32[32,1,256]{2,1,0:T(1,128)}), f32[32,1,256]{2,1,0:T(1,128)S(1)}, u32[]{:S(2)}, u32[]{:S(2)}) async-start(f32[32,1,256]{2,1,0:T(1,128)} %shard_map.60), calls=%async_computation.1 | async-start | bytes 65536 | tf_op jit(solution)/shard_map/all_to_all | solution.py:20
  38.5 12.1 %all-to-all-done.1 = f32[32,1,256]{2,1,0:T(1,128)S(1)} async-done(((f32[32,1,256]{2,1,0:T(1,128)}), f32[32,1,256]{2,1,0:T(1,128)S(1)}, u32[]{:S(2)}, u32[]{:S(2)}) %all-to-all-start.1) | async-done | bytes 32800 | tf_op jit(solution)/shard_map/all_to_all | solution.py:20
  50.6 0.1 reduce_sum.54
  50.7 0.1 fusion.4
  50.7 0.1 fusion.3
  50.9 10.2 %all_to_all.46 = bf16[16,64,128]{2,1,0:T(8,128)(2,1)S(1)} all-to-all(bf16[16,64,128]{2,1,0:T(8,128)(2,1)S(1)} %broadcast_in_dim.11), channel_id=1, replica_groups=mesh['gx_0'=4,'gx_1'=4,'gy_0'=16,'gy_1'=2] {'gx_0','gx_1'}, dimensions={0} | all-to-all | bytes 524288 | tf_op jit(solution)/shard_map/all_to_all | solution.py:20
  61.1 0.0 copy-done.2
  61.1 1.0 shard_map.62
  62.1 4.4 %collective-permute-start = (bf16[1024,128]{1,0:T(8,128)(2,1)S(1)}, bf16[1024,128]{1,0:T(8,128)(2,1)S(1)}, u32[]{:S(2)}, u32[]{:S(2)}) collective-permute-start(bf16[1024,128]{1,0:T(8,128)(2,1)S(1)} %shard_map.62), channel_id=1, source_target_pairs={{0,1},{1,0},{2,3},{3,2},{4,5},{5,4},{6,7},{7,6},{8,9},{9,8},{10,11... | collective-permute-start | bytes 786440 | tf_op jit(solution)/shard_map/ppermute | solution.py:180
  66.4 1.0 shard_map.61
  67.4 0.2 collective-permute-done
  67.6 0.1 add_convert_fusion.1
  67.6 10.7 %all_to_all.47 = bf16[16,64,128]{2,1,0:T(8,128)(2,1)S(1)} all-to-all(bf16[16,64,128]{2,1,0:T(8,128)(2,1)S(1)} %bitcast.37), channel_id=1, replica_groups=mesh['gx_0'=4,'gx_1'=4,'gy_0'=16,'gy_1'=2] {'gx_0','gx_1'}, dimensions={0} | all-to-all | bytes 524288 | tf_op jit(solution)/shard_map/all_to_all | solution.py:20
  78.4 15.4 %all_to_all.48 = bf16[16,64,128]{2,1,0:T(8,128)(2,1)S(1)} all-to-all(bf16[16,64,128]{2,1,0:T(8,128)(2,1)S(1)} %all_to_all.47), channel_id=1, replica_groups=mesh['gx_0'=4,'gx_1'=4,'gy_0'=16,'gy_1'=2] {'gy_0'}, dimensions={0} | all-to-all | bytes 524288 | tf_op jit(solution)/shard_map/all_to_all | solution.py:20
  93.8 0.1 multiply_reduce_fusion.1
  94.0 10.1 %all_to_all.49 = bf16[16,64,128]{2,1,0:T(8,128)(2,1)S(1)} all-to-all(bf16[16,64,128]{2,1,0:T(8,128)(2,1)S(1)} %broadcast_in_dim.12), channel_id=1, replica_groups=mesh['gx_0'=4,'gx_1'=4,'gy_0'=16,'gy_1'=2] {'gx_0','gx_1'}, dimensions={0} | all-to-all | bytes 524288 | tf_op jit(solution)/shard_map/all_to_all | solution.py:20
  104.1 1.1 shard_map.64
  105.2 10.0 %collective-permute-start.1 = (bf16[1024,128]{1,0:T(8,128)(2,1)S(1)}, bf16[1024,128]{1,0:T(8,128)(2,1)S(1)}, u32[]{:S(2)}, u32[]{:S(2)}) collective-permute-start(bf16[1024,128]{1,0:T(8,128)(2,1)S(1)} %shard_map.64), channel_id=1, source_target_pairs={{0,1},{1,0},{2,3},{3,2},{4,5},{5,4},{6,7},{7,6},{8,9},{9,8},{10,11... | collective-permute-start | bytes 786440 | tf_op jit(solution)/shard_map/ppermute | solution.py:180
  115.2 1.1 shard_map.63
  116.3 0.1 collective-permute-done.1
  116.3 0.1 add_convert_fusion
  116.4 18.9 %all_to_all.50 = bf16[16,64,128]{2,1,0:T(8,128)(2,1)S(1)} all-to-all(bf16[16,64,128]{2,1,0:T(8,128)(2,1)S(1)} %bitcast.38), channel_id=1, replica_groups=mesh['gx_0'=4,'gx_1'=4,'gy_0'=16,'gy_1'=2] {'gy_0'}, dimensions={0} | all-to-all | bytes 524288 | tf_op jit(solution)/shard_map/all_to_all | solution.py:20
  135.3 0.1 multiply_reduce_fusion
  135.4 15.4 %all_to_all.51 = f32[32,2,128]{2,1,0:T(2,128)S(1)} all-to-all(f32[32,2,128]{2,1,0:T(2,128)S(1)} %broadcast_in_dim.13), channel_id=1, replica_groups=mesh['gx_0'=4,'gx_1'=4,'gy_0'=16,'gy_1'=2] {'gx_0','gx_1','gy_1'}, dimensions={0} | all-to-all | bytes 65536 | tf_op jit(solution)/shard_map/all_to_all | solution.py:20
  150.9 16.8 %all_to_all.52.squares = f32[16,2,128]{2,1,0:T(2,128)S(1)} all-to-all(f32[16,2,128]{2,1,0:T(2,128)S(1)} %broadcast_in_dim.14), channel_id=1, replica_groups=mesh['gx_0'=4,'gx_1'=4,'gy_0'=16,'gy_1'=2] {'gy_0'}, dimensions={0} | all-to-all | bytes 32768 | tf_op jit(solution)/shard_map/all_to_all | solution.py:20
  167.7 0.7 shard_map.65
  (14 shorter events, 0.3 us)
Async XLA Ops:
  0.7 60.4 %copy-start.2 = (s32[16,1]{0,1:T(1,128)S(1)}, s32[16,1]{0,1:T(1,128)}, u32[]{:S(2)}) copy-start(s32[16,1]{0,1:T(1,128)} %param.6) | copy-start | bytes 196
  0.7 60.4 %copy-start.3 = (s32[16,3]{0,1:T(4,128)S(1)}, s32[16,3]{0,1:T(4,128)}, u32[]{:S(2)}) copy-start(s32[16,3]{0,1:T(4,128)} %param.5) | copy-start | bytes 580
  3.8 57.3 %copy-start = (bf16[16,3,128,128]{3,2,1,0:T(8,128)(2,1)S(1)}, bf16[16,3,128,128]{3,2,1,0:T(8,128)(2,1)}, u32[]{:S(2)}) copy-start(bf16[16,3,128,128]{3,2,1,0:T(8,128)(2,1)} %tiles.9) | copy-start | bytes 4718596
  19.4 0.7 copy-start.1
  20.8 29.8 %all-to-all-start.1 = ((f32[32,1,256]{2,1,0:T(1,128)}), f32[32,1,256]{2,1,0:T(1,128)S(1)}, u32[]{:S(2)}, u32[]{:S(2)}) async-start(f32[32,1,256]{2,1,0:T(1,128)} %shard_map.60), calls=%async_computation.1 | async-start | bytes 65536 | tf_op jit(solution)/shard_map/all_to_all | solution.py:20
  62.1 5.5 %collective-permute-start = (bf16[1024,128]{1,0:T(8,128)(2,1)S(1)}, bf16[1024,128]{1,0:T(8,128)(2,1)S(1)}, u32[]{:S(2)}, u32[]{:S(2)}) collective-permute-start(bf16[1024,128]{1,0:T(8,128)(2,1)S(1)} %shard_map.62), channel_id=1, source_target_pairs={{0,1},{1,0},{2,3},{3,2},{4,5},{5,4},{6,7},{7,6},{8,9},{9,8},{10,11... | collective-permute-start | bytes 786440 | tf_op jit(solution)/shard_map/ppermute | solution.py:180
  105.2 11.2 %collective-permute-start.1 = (bf16[1024,128]{1,0:T(8,128)(2,1)S(1)}, bf16[1024,128]{1,0:T(8,128)(2,1)S(1)}, u32[]{:S(2)}, u32[]{:S(2)}) collective-permute-start(bf16[1024,128]{1,0:T(8,128)(2,1)S(1)} %shard_map.64), channel_id=1, source_target_pairs={{0,1},{1,0},{2,3},{3,2},{4,5},{5,4},{6,7},{7,6},{8,9},{9,8},{10,11... | collective-permute-start | bytes 786440 | tf_op jit(solution)/shard_map/ppermute | solution.py:180
